TPU v7x, 256 devices: a whole 4x4x8 slice. The times are simulated.
256 devices in a mesh: dp: 2 (over z_lo), col: 16 (over y, z_hi), red: 8 (over x, core).
Axes of the slice: x: 4, y: 4, z: 8 (z_hi: 4, z_lo: 2; z = z_hi * 2 + z_lo), core: 2. Of those that a mesh axis runs over, the one named last changes fastest.
Arguments:
- inputs: bfloat16 [1024, 8192], P(('dp', 'col'), 'red'), may hold values from -6 to 6
- out_grad: bfloat16 [1024, 8192], P(('dp', 'col'), 'red'), may hold values from -1.5 to 1.5
- w_gate: bfloat16 [8192, 14336], P('red', 'col'), may hold values from -0.125 to 0.125
- w_up: bfloat16 [8192, 14336], P('red', 'col'), may hold values from -0.125 to 0.125
- w_down: bfloat16 [14336, 8192], P('col', 'red'), may hold values from -0.09375 to 0.09375
- block_mask: int32 [64, 112], P('red', 'col'), may hold values 0 or 1
Outputs:
- output: bfloat16 [1024, 8192], P(('dp', 'col'), 'red')
- input_grad: bfloat16 [1024, 8192], P(('dp', 'col'), 'red')
- grad_gate: bfloat16 [8192, 14336], P('red', 'col')
- grad_up: bfloat16 [8192, 14336], P('red', 'col')
- grad_down: bfloat16 [14336, 8192], P('col', 'red')
All inputs are finite; a program needn't handle non-finite values. No bound on the sum of `block_mask` on one device may be relied on, other than what follows from the above.
Results may differ from a plain program's by a relative error of at most 0.005.
Values may be sent and summed in bfloat16 or wider, within the bound.
No kernel may reach another device: no remote copies, remote signals or barrier semaphores. Data moves between devices by JAX's collectives and lax.ppermute only.
A program may use at most 128 MiB of HBM per device.

v0:
```python
import jax
import jax.numpy as jnp
from jax import lax
from jax.experimental import pallas as pl
from jax.experimental.pallas import tpu as pltpu
from jax.sharding import Mesh, PartitionSpec as P

BLK = 128
F32 = jnp.float32
BF16 = jnp.bfloat16

ROWS = (((1,), (1,)), ((), ()))
COLS = (((0,), (0,)), ((), ()))

PARTNERS = ((1, 3), (3, 1))


def exchange(value, axis, step):
    pairs = [(2 * i + c, 2 * (i ^ PARTNERS[c][step]) + c) for i in range(4) for c in range(2)]
    return lax.ppermute(value, (axis, "core"), pairs)


def swap(value, axis):
    return lax.ppermute(value, axis, [(0, 1), (1, 0)])


def after(value, *earlier):
    return lax.optimization_barrier((value, *earlier))[0]


def scalars():
    return pl.BlockSpec(memory_space=pltpu.SMEM)


def keep(flag, block):
    return jnp.where(flag > 0, block, jnp.zeros_like(block))


def row_pieces(first, own, near, rest):
    size = own.shape[0]
    other = rest[:size, :]
    return [own[...], jnp.where(first, near[...], other), jnp.where(first, other, near[...]), rest[size:, :]]


def acts_rows(side, two, rest, two_swapped, rest_swapped):
    pieces = [(two, two_swapped, 0), (two, two_swapped, 1), (rest, rest_swapped, 0), (rest, rest_swapped, 1)]
    return jnp.concatenate(
        [ref[k, side, y] for y in range(4) for mine, sibling, k in pieces for ref in (mine, sibling)], axis=0
    )


def call(kernel, outs, operands, flops, scratch=(), **grid):
    vmem = pl.BlockSpec(memory_space=pltpu.VMEM)
    return pl.pallas_call(
        kernel,
        in_specs=[scalars(), scalars(), *(vmem for _ in operands[2:])],
        out_specs=grid.pop("out_specs", [vmem] * len(outs)),
        out_shape=outs,
        scratch_shapes=list(scratch),
        compiler_params=pltpu.CompilerParams(vmem_limit_bytes=30 << 20),
        cost_estimate=pl.CostEstimate(flops=flops, bytes_accessed=1 << 20, transcendentals=0),
        **grid,
    )(*operands)


def blocks(count):
    return [slice(k * BLK, (k + 1) * BLK) for k in range(count)]


def masked(weight, rows, cols, flag):
    return jnp.concatenate(
        [
            jnp.concatenate(
                [keep(flag(r, c), weight[r * BLK : (r + 1) * BLK, c * BLK : (c + 1) * BLK]) for r in rows], axis=0
            )
            for c in cols
        ],
        axis=1,
    )


def split_rows(acc, side, cols, kept, sent):
    acc = acc.reshape(4, 4, 2, acc.shape[0] // 32, acc.shape[1])
    for k in range(4):
        kept[k, side, :, :, cols] = acc[:, k, 0]
        sent[k, side, :, :, cols] = acc[:, k, 1]


def gate_up_kernel(core, mask, own, near, rest, wg, wu, kept, sent):
    rows = jnp.concatenate(row_pieces(core[0] == 0, own, near, rest), axis=0)
    feat_blocks = range(wg.shape[0] // BLK)
    for j, cols in enumerate(blocks(wg.shape[1] // BLK)):
        weight = jnp.concatenate([masked(w, feat_blocks, [j], lambda r, c: mask[r, c]) for w in (wg, wu)], axis=1)
        pre = jnp.dot(rows, weight, preferred_element_type=F32)
        split_rows(pre[:, :BLK], 0, cols, kept, sent)
        split_rows(pre[:, BLK:], 1, cols, kept, sent)


def back_kernel(core, mask, own, near, rest, wd, kept, sent):
    rows = jnp.concatenate(row_pieces(core[0] == 0, own, near, rest), axis=0)
    hid_blocks, feat_blocks = wd.shape[0] // BLK, range(wd.shape[1] // BLK)
    for j in range(0, hid_blocks, 2):
        stop = min(j + 2, hid_blocks)
        weight = masked(wd, range(j, stop), feat_blocks, lambda r, c: mask[c, r])
        acc = lax.dot_general(rows, weight, ROWS, preferred_element_type=F32)
        split_rows(acc, 0, slice(j * BLK, stop * BLK), kept, sent)


def partial_sums(kernel, core, mask, pieces, weights, hid):
    tok, feats = 4 * pieces[0].shape[0], pieces[0].shape[1]
    sides = len(weights)
    shape = jax.ShapeDtypeStruct((4, sides, 4, tok // 32, hid), F32)
    return call(kernel, [shape, shape], (core, mask, *pieces, *weights), 2 * sides * tok * feats * hid)


def outputs_kernel(core, mask, two, rest, two_swapped, rest_swapped, wg, wu, wd, kept, sent):
    hidden, gate, up = (acts_rows(side, two, rest, two_swapped, rest_swapped) for side in range(3))
    first = core[0] == 0
    feat_blocks, hid_blocks = wg.shape[0] // BLK, range(wg.shape[1] // BLK)
    for i in range(0, feat_blocks, 2):
        span = range(i, min(i + 2, feat_blocks))
        cols = slice(i * BLK, span.stop * BLK)
        down = masked(wd, hid_blocks, span, lambda r, c: mask[c, r])
        output = jnp.dot(hidden, down, preferred_element_type=F32)
        grad = sum(
            lax.dot_general(
                value, masked(w, span, hid_blocks, lambda r, c: mask[r, c]), ROWS, preferred_element_type=F32
            )
            for value, w in ((gate, wg), (up, wu))
        )
        for side, value in enumerate((output, grad)):
            value = value.reshape(4, -1, value.shape[1])
            kept[0, side, :, cols] = value[0]
            kept[1, side, :, cols] = jnp.where(first, value[2], value[1])
            sent[0, side, :, cols] = jnp.where(first, value[1], value[2]).astype(BF16)
            sent[1, side, :, cols] = value[3].astype(BF16)


def outputs(core, mask, acts, w_gate, w_up, w_down):
    hid, feats = w_down.shape
    tok = 32 * acts[0].shape[3]
    shape = (2, 2, tok // 4, feats)
    outs = [jax.ShapeDtypeStruct(shape, F32), jax.ShapeDtypeStruct(shape, BF16)]
    return call(outputs_kernel, outs, (core, mask, *acts, w_gate, w_up, w_down), 6 * tok * hid * feats)


def own_grads_kernel(core, mask, *refs):
    tokens, cots, acts, both, down = refs[:3], refs[3:6], refs[6:10], refs[10], refs[11]
    first = core[0] == 0
    tok_t = jnp.concatenate(row_pieces(first, *tokens), axis=0).T
    cot = jnp.concatenate(row_pieces(first, *cots), axis=0)
    for j, cols in enumerate(blocks(acts[0].shape[-1] // BLK)):
        hidden, gate, up = (acts_rows(side, *(ref.at[:, :, :, :, cols] for ref in acts)) for side in range(3))
        both[j] = jnp.dot(tok_t, jnp.concatenate([gate, up], axis=1), preferred_element_type=F32)
        down[cols, :] = lax.dot_general(hidden, cot, COLS, preferred_element_type=F32)


def own_grads(core, mask, tokens, cots, acts):
    feats, hid, count = tokens[0].shape[1], acts[0].shape[-1], 4 * tokens[0].shape[0]
    outs = [
        jax.ShapeDtypeStruct((hid // BLK, feats, 2 * BLK), F32),
        jax.ShapeDtypeStruct((hid, feats), F32),
    ]
    return call(own_grads_kernel, outs, (core, mask, *tokens, *cots, *acts), 6 * count * feats * hid)


def all_grads_kernel(core, mask, *refs):
    theirs, acts, own_both, own_down = refs[:3], refs[3:7], refs[7], refs[8]
    grad_gate, grad_up, grad_down, tok_t, cot = refs[9:]
    j = pl.program_id(0)
    feats = tok_t.shape[0]

    @pl.when(j == 0)
    def _():
        rows = jnp.concatenate(row_pieces(core[0] == 0, *theirs), axis=0)
        tok_t[...] = rows[:, :feats].T
        cot[...] = rows[:, feats:]

    cols = pl.ds(pl.multiple_of(j * BLK, BLK), BLK)
    hidden, gate, up = (acts_rows(side, *(ref.at[:, :, :, :, cols] for ref in acts)) for side in range(3))
    both = jnp.dot(tok_t[...], jnp.concatenate([gate, up], axis=1), preferred_element_type=F32)
    both = (both + own_both[j]).astype(BF16)
    down = lax.dot_general(hidden, cot[...], COLS, preferred_element_type=F32)
    down = (down + own_down[cols, :]).astype(BF16)
    for k, spot in enumerate(blocks(feats // BLK)):
        grad_gate[spot, :] = keep(mask[k, j], both[spot, :BLK])
        grad_up[spot, :] = keep(mask[k, j], both[spot, BLK:])
        grad_down[:, spot] = keep(mask[k, j], down[:, spot])


def all_grads(core, mask, theirs, acts, own):
    feats, hid, count = theirs[0].shape[1] // 2, acts[0].shape[-1], 4 * theirs[0].shape[0]
    up = jax.ShapeDtypeStruct((feats, hid), BF16)
    up_tile = pl.BlockSpec((feats, BLK), lambda j: (0, j))
    return call(
        all_grads_kernel,
        [up, up, jax.ShapeDtypeStruct((hid, feats), BF16)],
        (core, mask, *theirs, *acts, *own),
        6 * count * feats * hid,
        [pltpu.VMEM((feats, count), BF16), pltpu.VMEM((count, feats), BF16)],
        grid=(hid // BLK,),
        out_specs=[up_tile, up_tile, pl.BlockSpec((BLK, feats), lambda j: (j, 0))],
    )


def frame(rows):
    quad = rows // 8
    x, z, core = lax.axis_index("x"), lax.axis_index("zh"), lax.axis_index("core")
    steps = jnp.array([[0, 1, 3, 2], [0, 3, 1, 2]], jnp.int32)
    spot = jnp.arange(4 * rows, dtype=jnp.int32)
    k, j, at_z, q = spot // rows, spot // (4 * quad) % 2, spot // quad % 4, spot % quad
    owner = core ^ j
    at_x = x ^ jnp.where(owner == 0, steps[0][k], steps[1][k])
    away = at_z ^ z
    piece = jnp.where(away == 0, 0, jnp.where(away == 2, 3, jnp.where((away == 1) == (core == 0), 1, 2)))
    wanted = piece * rows + (at_x * 2 + owner) * quad + q
    return (wanted[:, None] == spot[None, :]).astype(F32)


def gather(own, axis, wrap=jnp.concatenate):
    two = wrap([own, exchange(own, axis, 0)])
    return two, exchange(two, axis, 1)


def scatter(kept, sent, axis, *earlier):
    both = kept + exchange(sent, axis, 0).astype(F32)
    return both[0] + exchange(after(both[1].astype(BF16), *earlier), axis, 1).astype(F32)


def local(inputs, out_grad, w_gate, w_up, w_down, block_mask):
    rows, feats = inputs.shape
    hid = w_gate.shape[1]
    core = lax.axis_index("core").astype(jnp.int32).reshape(1)
    pick = frame(rows)

    def pick_rows(two, rest):
        z_rows = jnp.concatenate([two, rest], axis=0)
        return jnp.dot(pick.astype(BF16), z_rows, preferred_element_type=F32).astype(BF16)

    tok, cot = inputs, out_grad
    tok_near, cot_near = exchange(tok, "zh", 0), exchange(cot, "zh", 0)
    tok = after(jnp.concatenate([tok, tok_near], axis=0), cot_near)
    cot = jnp.concatenate([cot, cot_near], axis=0)
    tok, cot = pick_rows(tok, exchange(tok, "zh", 1)), pick_rows(cot, exchange(cot, "zh", 1))
    tok_near, cot_near = exchange(tok, "y", 0), exchange(cot, "y", 0)
    tok_rest = exchange(after(jnp.concatenate([tok, tok_near], axis=0), cot), "y", 1)
    cot_rest = exchange(jnp.concatenate([cot, cot_near], axis=0), "y", 1)
    tokens, cots = (tok, tok_near, tok_rest), (cot, cot_near, cot_rest)
    their_z = swap(jnp.concatenate([tok, cot], axis=1), "dp")

    pieces = (tok, tok_near, after(tok_rest, cot_near))
    pre_kept, pre_sent = partial_sums(gate_up_kernel, core, block_mask, pieces, (w_gate, w_up), hid)
    pre_got = swap(pre_sent, "core")
    pieces = (cot, cot_near, after(cot_rest, their_z))
    back_kept, back_sent = partial_sums(back_kernel, core, block_mask, pieces, (w_down,), hid)
    their_near = exchange(their_z, "y", 0)

    pre = pre_kept + pre_got
    back = back_kept + swap(back_sent, "core")
    kept = jnp.stack([jnp.concatenate([pre[k], back[k]]) for k in (0, 2)])
    sent = jnp.stack([jnp.concatenate([pre[k].astype(BF16), back[k].astype(BF16)]) for k in (1, 3)])
    gate_pre, up_pre, hidden_grad = scatter(kept, sent, "x", their_near)
    sig = jax.nn.sigmoid(gate_pre)
    hidden = (gate_pre * sig * up_pre).astype(BF16)
    gate_grad = (hidden_grad * up_pre * sig * (1.0 + gate_pre * (1.0 - sig))).astype(BF16)
    up_grad = (hidden_grad * gate_pre * sig).astype(BF16)
    own_acts = jnp.stack([hidden, gate_grad, up_grad])

    pair, far = gather(own_acts, "x", jnp.stack)
    their_acts = swap(own_acts, "dp")
    far = after(far, their_acts)
    acts = (pair, far, swap(pair, "core"), swap(far, "core"))
    their_rest = exchange(jnp.concatenate([their_z, their_near], axis=0), "y", 1)

    kept, sent = outputs(core, block_mask, acts, w_gate, w_up, w_down)
    their_pair = jnp.stack([their_acts, exchange(after(their_acts, far), "x", 0)])
    own = own_grads(core, block_mask, tokens, cots, acts)
    their_far = exchange(their_pair, "x", 1)
    both = kept + after(exchange(after(sent, their_rest), "y", 0)).astype(F32)
    second = exchange(after(both[1].astype(BF16), their_pair), "y", 1)
    total = both[0] + second.astype(F32)

    total = after(total, their_far)
    total = jnp.concatenate(
        [lax.dot_general(pick, side, COLS, precision="highest", preferred_element_type=F32) for side in total], axis=1
    ).reshape(4, rows, 2 * feats)
    kept, sent = jnp.stack([total[0], total[2]]), jnp.stack([total[1], total[3]]).astype(BF16)
    theirs = (their_z, their_near, their_rest)
    their_acts = (their_pair, their_far, swap(their_pair, "core"), swap(their_far, "core"))
    grads = all_grads(core, block_mask, theirs, their_acts, own)
    total = scatter(kept, sent, "zh", grads[0]).astype(BF16)
    return total[:, :feats], total[:, feats:], *grads


def solution(mesh):
    split = Mesh(mesh.devices.reshape(2, 4, 4, 4, 2), ("dp", "y", "zh", "x", "core"))
    token_rows = P(("dp", "y", "zh"), ("x", "core"))
    weight_in = P(("x", "core"), ("y", "zh"))
    weight_out = P(("y", "zh"), ("x", "core"))
    return jax.shard_map(
        local,
        mesh=split,
        in_specs=(token_rows, token_rows, weight_in, weight_in, weight_out, weight_in),
        out_specs=(token_rows, token_rows, weight_in, weight_in, weight_out),
        check_vma=False,
    )
```

profile of v0, /device:TPU:56, one launch (start us, length us, event | category | flops | bytes accessed | tf_op | source)
XLA Modules:
  0.0 150.5 jit_solution(14808897893202492538)
XLA Ops:
  0.6 3.4 %collective-permute-start = (bf16[32,1024]{1,0:T(8,128)(2,1)}, bf16[32,1024]{1,0:T(8,128)(2,1)S(1)}, u32[]{:S(2)}, u32[]{:S(2)}) collective-permute-start(bf16[32,1024]{1,0:T(8,128)(2,1)} %param.7), channel_id=1, source_target_pairs={{0,8},{1,25},{8,0},{9,17},{16,24},{17,9},{24,16},{25,1},{2,10},{3,... | collective-permute-start | bytes 196616 | tf_op jit(solution)/shard_map/ppermute | solution.py:20
  4.1 2.9 %collective-permute-done = bf16[32,1024]{1,0:T(8,128)(2,1)S(1)} collective-permute-done((bf16[32,1024]{1,0:T(8,128)(2,1)}, bf16[32,1024]{1,0:T(8,128)(2,1)S(1)}, u32[]{:S(2)}, u32[]{:S(2)}) %collective-permute-start) | collective-permute-done | bytes 65568 | tf_op jit(solution)/shard_map/ppermute | solution.py:20
  9.4 3.8 %collective-permute-start.2 = (bf16[64,1024]{1,0:T(8,128)(2,1)S(1)}, bf16[64,1024]{1,0:T(8,128)(2,1)S(1)}, u32[]{:S(2)}, u32[]{:S(2)}) collective-permute-start(bf16[64,1024]{1,0:T(8,128)(2,1)S(1)} %pad_maximum_fusion.10), channel_id=1, source_target_pairs={{0,24},{1,9},{8,16},{9,1},{16,8},{17,25},{24,0},{25,17},{2,26},{3,... | collective-permute-start | bytes 393224 | tf_op jit(solution)/shard_map/ppermute | solution.py:20
  14.5 2.5 %collective-permute-done.2 = bf16[64,1024]{1,0:T(8,128)(2,1)S(1)} collective-permute-done((bf16[64,1024]{1,0:T(8,128)(2,1)S(1)}, bf16[64,1024]{1,0:T(8,128)(2,1)S(1)}, u32[]{:S(2)}, u32[]{:S(2)}) %collective-permute-start.2) | collective-permute-done | bytes 131104 | tf_op jit(solution)/shard_map/ppermute | solution.py:20
  18.1 3.1 %collective-permute-done.4 = bf16[64,1024]{1,0:T(8,128)(2,1)S(1)} collective-permute-done((bf16[64,1024]{1,0:T(8,128)(2,1)S(1)}, bf16[64,1024]{1,0:T(8,128)(2,1)S(1)}, u32[]{:S(2)}, u32[]{:S(2)}) %collective-permute-start.4) | collective-permute-done | bytes 131104 | tf_op jit(solution)/shard_map/ppermute | solution.py:20
  27.0 6.2 %collective-permute-done.6.near.refs_4_ = bf16[128,1024]{1,0:T(8,128)(2,1)S(1)} collective-permute-done((bf16[128,1024]{1,0:T(8,128)(2,1)S(1)}, bf16[128,1024]{1,0:T(8,128)(2,1)S(1)}, u32[]{:S(2)}, u32[]{:S(2)}) %collective-permute-start.6) | collective-permute-done | bytes 262176 | tf_op jit(solution)/shard_map/ppermute | solution.py:20
  33.2 3.0 %collective-permute-start.8 = (bf16[256,1024]{1,0:T(8,128)(2,1)S(1)}, bf16[256,1024]{1,0:T(8,128)(2,1)S(1)}, u32[]{:S(2)}, u32[]{:S(2)}) collective-permute-start(bf16[256,1024]{1,0:T(8,128)(2,1)S(1)} %pad_maximum_fusion.6), channel_id=1, source_target_pairs={{0,96},{1,33},{32,64},{33,1},{64,32},{65,97},{96,0},{97,65},{2,98}... | collective-permute-start | bytes 1572872 | tf_op jit(solution)/shard_map/ppermute | solution.py:20
  37.1 2.7 %shard_map.110 = (f32[4,2,4,16,896]{4,3,2,1,0:T(8,128)S(1)}, f32[4,2,4,16,896]{4,3,2,1,0:T(8,128)S(1)}) custom-call(s32[1]{0:T(128)} %bitcast.2.core, s32[8,7]{1,0:T(8,128)S(1)} %copy-done, bf16[128,1024]{1,0:T(8,128)(2,1)S(1)} %convolution_convert_fusion.1.own.refs_0_, bf16[128,1024]{1,0:T(8,128)(2,1)S(1)} %collective-permute-done.3.near.refs_1_, ...), custom_call_target="tpu_custom_call" | custom-call | flops 1879048192 | bytes 1048576 | tf_op jit(solution)/shard_map/pallas_call | solution.py:54
  39.9 3.7 %collective-permute-done.8.rest.refs_5_ = bf16[256,1024]{1,0:T(8,128)(2,1)S(1)} collective-permute-done((bf16[256,1024]{1,0:T(8,128)(2,1)S(1)}, bf16[256,1024]{1,0:T(8,128)(2,1)S(1)}, u32[]{:S(2)}, u32[]{:S(2)}) %collective-permute-start.8) | collective-permute-done | bytes 524320 | tf_op jit(solution)/shard_map/ppermute | solution.py:20
  50.7 9.1 %collective-permute-done.11 = bf16[2,3,4,16,896]{4,3,2,1,0:T(8,128)(2,1)S(1)} collective-permute-done((bf16[2,3,4,16,896]{4,3,2,1,0:T(8,128)(2,1)S(1)}, bf16[2,3,4,16,896]{4,3,2,1,0:T(8,128)(2,1)S(1)}, u32[]{:S(2)}, u32[]{:S(2)}) %collective-permute-start.11) | collective-permute-done | bytes 688160 | tf_op jit(solution)/shard_map/ppermute | solution.py:20
  60.0 3.1 %collective-permute-start.13 = (bf16[3,4,16,896]{3,2,1,0:T(8,128)(2,1)S(1)}, bf16[3,4,16,896]{3,2,1,0:T(8,128)(2,1)S(1)}, u32[]{:S(2)}, u32[]{:S(2)}) collective-permute-start(bf16[3,4,16,896]{3,2,1,0:T(8,128)(2,1)S(1)} %fusion.10), channel_id=1, source_target_pairs={{0,6},{1,3},{2,4},{3,1},{4,2},{5,7},{6,0},{7,5},{8,14},{9,11},{10,... | collective-permute-start | bytes 1032200 | tf_op jit(solution)/shard_map/ppermute | solution.py:20
  63.2 5.6 %collective-permute-done.13 = bf16[3,4,16,896]{3,2,1,0:T(8,128)(2,1)S(1)} collective-permute-done((bf16[3,4,16,896]{3,2,1,0:T(8,128)(2,1)S(1)}, bf16[3,4,16,896]{3,2,1,0:T(8,128)(2,1)S(1)}, u32[]{:S(2)}, u32[]{:S(2)}) %collective-permute-start.13) | collective-permute-done | bytes 344096 | tf_op jit(solution)/shard_map/ppermute | solution.py:20
  69.5 6.8 %collective-permute-done.14 = bf16[3,4,16,896]{3,2,1,0:T(8,128)(2,1)S(1)} collective-permute-done((bf16[3,4,16,896]{3,2,1,0:T(8,128)(2,1)S(1)}, bf16[3,4,16,896]{3,2,1,0:T(8,128)(2,1)S(1)}, u32[]{:S(2)}, u32[]{:S(2)}) %collective-permute-start.14) | collective-permute-done | bytes 344096 | tf_op jit(solution)/shard_map/ppermute | solution.py:20
  76.4 3.0 %collective-permute-start.15 = (bf16[2,3,4,16,896]{4,3,2,1,0:T(8,128)(2,1)S(1)}, bf16[2,3,4,16,896]{4,3,2,1,0:T(8,128)(2,1)S(1)}, u32[]{:S(2)}, u32[]{:S(2)}) collective-permute-start(bf16[2,3,4,16,896]{4,3,2,1,0:T(8,128)(2,1)S(1)} %pad_maximum_fusion.3.two.refs_6_), channel_id=1, source_target_pairs={{0,6},{1,3},{2,4},{3,1},{4,2},{5,7},{6,0},{7,5},{8,14},{9,11},{10,... | collective-permute-start | bytes 2064392 | tf_op jit(solution)/shard_map/ppermute | solution.py:20
  82.8 3.8 %collective-permute-done.16 = bf16[3,4,16,896]{3,2,1,0:T(8,128)(2,1)S(1)} collective-permute-done((bf16[3,4,16,896]{3,2,1,0:T(8,128)(2,1)S(1)}, bf16[3,4,16,896]{3,2,1,0:T(8,128)(2,1)S(1)}, u32[]{:S(2)}, u32[]{:S(2)}) %collective-permute-start.16) | collective-permute-done | bytes 344096 | tf_op jit(solution)/shard_map/ppermute | solution.py:24
  90.8 4.1 %shard_map.112 = (f32[2,2,128,1024]{3,2,1,0:T(8,128)S(1)}, bf16[2,2,128,1024]{3,2,1,0:T(8,128)(2,1)S(1)}) custom-call(s32[1]{0:T(128)} %bitcast.2.core, s32[8,7]{1,0:T(8,128)S(1)} %copy-done, bf16[2,3,4,16,896]{4,3,2,1,0:T(8,128)(2,1)S(1)} %pad_maximum_fusion.3.two.refs_6_, bf16[2,3,4,16,896]{4,3,2,1,0:T(8,128)(2,1)S(1)} %collective-permute-done.15.rest.refs_7_, ...), custom_call_target="tpu_custom_call" | custom-call | flops 2818572288 | bytes 1048576 | tf_op jit(solution)/shard_map/pallas_call | solution.py:54
  94.9 2.6 %collective-permute-done.19.refs_2_ = bf16[256,2048]{1,0:T(8,128)(2,1)S(1)} collective-permute-done((bf16[256,2048]{1,0:T(8,128)(2,1)S(1)}, bf16[256,2048]{1,0:T(8,128)(2,1)S(1)}, u32[]{:S(2)}, u32[]{:S(2)}) %collective-permute-start.19) | collective-permute-done | bytes 1048608 | tf_op jit(solution)/shard_map/ppermute | solution.py:20
  97.5 7.2 %collective-permute-done.21 = bf16[3,4,16,896]{3,2,1,0:T(8,128)(2,1)S(1)} collective-permute-done((bf16[3,4,16,896]{3,2,1,0:T(8,128)(2,1)S(1)}, bf16[3,4,16,896]{3,2,1,0:T(8,128)(2,1)S(1)}, u32[]{:S(2)}, u32[]{:S(2)}) %collective-permute-start.21) | collective-permute-done | bytes 344096 | tf_op jit(solution)/shard_map/ppermute | solution.py:20
  105.4 6.9 %collective-permute-done.20 = bf16[2,2,128,1024]{3,2,1,0:T(8,128)(2,1)S(1)} collective-permute-done((bf16[2,2,128,1024]{3,2,1,0:T(8,128)(2,1)S(1)}, bf16[2,2,128,1024]{3,2,1,0:T(8,128)(2,1)S(1)}, u32[]{:S(2)}, u32[]{:S(2)}) %collective-permute-start.20) | collective-permute-done | bytes 1048608 | tf_op jit(solution)/shard_map/ppermute | solution.py:20
  114.1 3.7 %shard_map.113 = (f32[7,1024,256]{2,1,0:T(8,128)S(1)}, f32[896,1024]{1,0:T(8,128)S(1)}) custom-call(s32[1]{0:T(128)} %bitcast.2.core, s32[8,7]{1,0:T(8,128)S(1)} %copy-done, bf16[128,1024]{1,0:T(8,128)(2,1)S(1)} %convolution_convert_fusion.1.own.refs_0_, bf16[128,1024]{1,0:T(8,128)(2,1)S(1)} %collective-permute-done.3.near.refs_1_, ...), custom_call_target="tpu_custom_call" | custom-call | flops 2818572288 | bytes 1048576 | tf_op jit(solution)/shard_map/pallas_call | solution.py:54
  118.4 4.7 %collective-permute-done.22 = bf16[2,128,1024]{2,1,0:T(8,128)(2,1)S(1)} collective-permute-done((bf16[2,128,1024]{2,1,0:T(8,128)(2,1)S(1)}, bf16[2,128,1024]{2,1,0:T(8,128)(2,1)S(1)}, u32[]{:S(2)}, u32[]{:S(2)}) %collective-permute-start.22) | collective-permute-done | bytes 524320 | tf_op jit(solution)/shard_map/ppermute | solution.py:20
  125.8 7.0 %shard_map.114 = (bf16[1024,896]{1,0:T(8,128)(2,1)}, bf16[1024,896]{1,0:T(8,128)(2,1)}, bf16[896,1024]{1,0:T(8,128)(2,1)}) custom-call(s32[1]{0:T(128)} %bitcast.2.core, s32[8,7]{1,0:T(8,128)S(1)} %copy-done, bf16[128,2048]{1,0:T(8,128)(2,1)S(1)} %collective-permute-done.9.refs_0_, bf16[128,2048]{1,0:T(8,128)(2,1)S(1)} %collective-permute-done.12.refs_1_, ...), custom_call_target="tpu_custom_call" | custom-call | flops 2818572288 | bytes 1048576 | tf_op jit(solution)/shard_map/pallas_call | solution.py:54
  132.9 14.0 %collective-permute-start.27 = (bf16[32,2048]{1,0:T(8,128)(2,1)S(1)}, bf16[32,2048]{1,0:T(8,128)(2,1)S(1)}, u32[]{:S(2)}, u32[]{:S(2)}) collective-permute-start(bf16[32,2048]{1,0:T(8,128)(2,1)S(1)} %fusion.25), channel_id=1, source_target_pairs={{0,24},{1,9},{8,16},{9,1},{16,8},{17,25},{24,0},{25,17},{2,26},{3,... | collective-permute-start | bytes 393224 | tf_op jit(solution)/shard_map/ppermute | solution.py:20
  146.8 2.9 %collective-permute-done.27 = bf16[32,2048]{1,0:T(8,128)(2,1)S(1)} collective-permute-done((bf16[32,2048]{1,0:T(8,128)(2,1)S(1)}, bf16[32,2048]{1,0:T(8,128)(2,1)S(1)}, u32[]{:S(2)}, u32[]{:S(2)}) %collective-permute-start.27) | collective-permute-done | bytes 131104 | tf_op jit(solution)/shard_map/ppermute | solution.py:20
  (83 shorter events, 33.6 us)
Async XLA Ops:
  0.6 6.3 %collective-permute-start = (bf16[32,1024]{1,0:T(8,128)(2,1)}, bf16[32,1024]{1,0:T(8,128)(2,1)S(1)}, u32[]{:S(2)}, u32[]{:S(2)}) collective-permute-start(bf16[32,1024]{1,0:T(8,128)(2,1)} %param.7), channel_id=1, source_target_pairs={{0,8},{1,25},{8,0},{9,17},{16,24},{17,9},{24,16},{25,1},{2,10},{3,... | collective-permute-start | bytes 196616 | tf_op jit(solution)/shard_map/ppermute | solution.py:20
  9.4 7.6 %collective-permute-start.2 = (bf16[64,1024]{1,0:T(8,128)(2,1)S(1)}, bf16[64,1024]{1,0:T(8,128)(2,1)S(1)}, u32[]{:S(2)}, u32[]{:S(2)}) collective-permute-start(bf16[64,1024]{1,0:T(8,128)(2,1)S(1)} %pad_maximum_fusion.10), channel_id=1, source_target_pairs={{0,24},{1,9},{8,16},{9,1},{16,8},{17,25},{24,0},{25,17},{2,26},{3,... | collective-permute-start | bytes 393224 | tf_op jit(solution)/shard_map/ppermute | solution.py:20
  14.0 7.2 %collective-permute-start.4 = (bf16[64,1024]{1,0:T(8,128)(2,1)S(1)}, bf16[64,1024]{1,0:T(8,128)(2,1)S(1)}, u32[]{:S(2)}, u32[]{:S(2)}) collective-permute-start(bf16[64,1024]{1,0:T(8,128)(2,1)S(1)} %pad_maximum_fusion.11), channel_id=1, source_target_pairs={{0,24},{1,9},{8,16},{9,1},{16,8},{17,25},{24,0},{25,17},{2,26},{3,... | collective-permute-start | bytes 393224 | tf_op jit(solution)/shard_map/ppermute | solution.py:20
  17.3 6.5 %collective-permute-start.3 = (bf16[128,1024]{1,0:T(8,128)(2,1)S(1)}, bf16[128,1024]{1,0:T(8,128)(2,1)S(1)}, u32[]{:S(2)}, u32[]{:S(2)}) collective-permute-start(bf16[128,1024]{1,0:T(8,128)(2,1)S(1)} %convolution_convert_fusion.1.own.refs_0_), channel_id=1, source_target_pairs={{0,32},{1,97},{32,0},{33,65},{64,96},{65,33},{96,64},{97,1},{2,34}... | collective-permute-start | bytes 786440 | tf_op jit(solution)/shard_map/ppermute | solution.py:20
  23.8 13.3 %collective-permute-start.5 = (bf16[256,1024]{1,0:T(8,128)(2,1)S(1)}, bf16[256,1024]{1,0:T(8,128)(2,1)S(1)}, u32[]{:S(2)}, u32[]{:S(2)}) collective-permute-start(bf16[256,1024]{1,0:T(8,128)(2,1)S(1)} %pad_maximum_fusion.5), channel_id=1, source_target_pairs={{0,96},{1,33},{32,64},{33,1},{64,32},{65,97},{96,0},{97,65},{2,98}... | collective-permute-start | bytes 1572872 | tf_op jit(solution)/shard_map/ppermute | solution.py:20
  24.0 9.2 %collective-permute-start.6 = (bf16[128,1024]{1,0:T(8,128)(2,1)S(1)}, bf16[128,1024]{1,0:T(8,128)(2,1)S(1)}, u32[]{:S(2)}, u32[]{:S(2)}) collective-permute-start(bf16[128,1024]{1,0:T(8,128)(2,1)S(1)} %convolution_convert_fusion.own.refs_3_), channel_id=1, source_target_pairs={{0,32},{1,97},{32,0},{33,65},{64,96},{65,33},{96,64},{97,1},{2,34}... | collective-permute-start | bytes 786440 | tf_op jit(solution)/shard_map/ppermute | solution.py:20
  25.1 14.8 %collective-permute-start.9 = (bf16[128,2048]{1,0:T(8,128)(2,1)S(1)}, bf16[128,2048]{1,0:T(8,128)(2,1)S(1)}, u32[]{:S(2)}, u32[]{:S(2)}) collective-permute-start(bf16[128,2048]{1,0:T(8,128)(2,1)S(1)} %pad_maximum_fusion.7), channel_id=1, source_target_pairs={{0,128},{128,0},{1,129},{129,1},{2,130},{130,2},{3,131},{131,3},{4... | collective-permute-start | bytes 1572872 | tf_op jit(solution)/shard_map/ppermute | solution.py:24
  33.2 10.5 %collective-permute-start.8 = (bf16[256,1024]{1,0:T(8,128)(2,1)S(1)}, bf16[256,1024]{1,0:T(8,128)(2,1)S(1)}, u32[]{:S(2)}, u32[]{:S(2)}) collective-permute-start(bf16[256,1024]{1,0:T(8,128)(2,1)S(1)} %pad_maximum_fusion.6), channel_id=1, source_target_pairs={{0,96},{1,33},{32,64},{33,1},{64,32},{65,97},{96,0},{97,65},{2,98}... | collective-permute-start | bytes 1572872 | tf_op jit(solution)/shard_map/ppermute | solution.py:20
  39.8 8.5 %collective-permute-start.7 = (f32[4,2,4,16,896]{4,3,2,1,0:T(8,128)S(1)}, f32[4,2,4,16,896]{4,3,2,1,0:T(8,128)S(1)}, u32[]{:S(2)}, u32[]{:S(2)}) collective-permute-start(f32[4,2,4,16,896]{4,3,2,1,0:T(8,128)S(1)} %get-tuple-element.31), channel_id=1, source_target_pairs={{0,1},{1,0},{2,3},{3,2},{4,5},{5,4},{6,7},{7,6},{8,9},{9,8},{10,11... | collective-permute-start | bytes 5505032 | tf_op jit(solution)/shard_map/ppermute | solution.py:24
  48.8 11.0 %collective-permute-start.11 = (bf16[2,3,4,16,896]{4,3,2,1,0:T(8,128)(2,1)S(1)}, bf16[2,3,4,16,896]{4,3,2,1,0:T(8,128)(2,1)S(1)}, u32[]{:S(2)}, u32[]{:S(2)}) collective-permute-start(bf16[2,3,4,16,896]{4,3,2,1,0:T(8,128)(2,1)S(1)} %pad_maximum_fusion.2), channel_id=1, source_target_pairs={{0,2},{1,7},{2,0},{3,5},{4,6},{5,3},{6,4},{7,1},{8,10},{9,15},{10,... | collective-permute-start | bytes 2064392 | tf_op jit(solution)/shard_map/ppermute | solution.py:20
  50.5 9.5 %collective-permute-start.12 = (bf16[128,2048]{1,0:T(8,128)(2,1)S(1)}, bf16[128,2048]{1,0:T(8,128)(2,1)S(1)}, u32[]{:S(2)}, u32[]{:S(2)}) collective-permute-start(bf16[128,2048]{1,0:T(8,128)(2,1)S(1)} %collective-permute-done.9.refs_0_), channel_id=1, source_target_pairs={{0,32},{1,97},{32,0},{33,65},{64,96},{65,33},{96,64},{97,1},{2,34}... | collective-permute-start | bytes 1572872 | tf_op jit(solution)/shard_map/ppermute | solution.py:20
  60.0 8.7 %collective-permute-start.13 = (bf16[3,4,16,896]{3,2,1,0:T(8,128)(2,1)S(1)}, bf16[3,4,16,896]{3,2,1,0:T(8,128)(2,1)S(1)}, u32[]{:S(2)}, u32[]{:S(2)}) collective-permute-start(bf16[3,4,16,896]{3,2,1,0:T(8,128)(2,1)S(1)} %fusion.10), channel_id=1, source_target_pairs={{0,6},{1,3},{2,4},{3,1},{4,2},{5,7},{6,0},{7,5},{8,14},{9,11},{10,... | collective-permute-start | bytes 1032200 | tf_op jit(solution)/shard_map/ppermute | solution.py:20
  69.0 7.3 %collective-permute-start.14 = (bf16[3,4,16,896]{3,2,1,0:T(8,128)(2,1)S(1)}, bf16[3,4,16,896]{3,2,1,0:T(8,128)(2,1)S(1)}, u32[]{:S(2)}, u32[]{:S(2)}) collective-permute-start(bf16[3,4,16,896]{3,2,1,0:T(8,128)(2,1)S(1)} %get-tuple-element.69), channel_id=1, source_target_pairs={{0,2},{1,7},{2,0},{3,5},{4,6},{5,3},{6,4},{7,1},{8,10},{9,15},{10,... | collective-permute-start | bytes 1032200 | tf_op jit(solution)/shard_map/ppermute | solution.py:20
  76.4 12.2 %collective-permute-start.15 = (bf16[2,3,4,16,896]{4,3,2,1,0:T(8,128)(2,1)S(1)}, bf16[2,3,4,16,896]{4,3,2,1,0:T(8,128)(2,1)S(1)}, u32[]{:S(2)}, u32[]{:S(2)}) collective-permute-start(bf16[2,3,4,16,896]{4,3,2,1,0:T(8,128)(2,1)S(1)} %pad_maximum_fusion.3.two.refs_6_), channel_id=1, source_target_pairs={{0,6},{1,3},{2,4},{3,1},{4,2},{5,7},{6,0},{7,5},{8,14},{9,11},{10,... | collective-permute-start | bytes 2064392 | tf_op jit(solution)/shard_map/ppermute | solution.py:20
  79.4 7.2 %collective-permute-start.16 = (bf16[3,4,16,896]{3,2,1,0:T(8,128)(2,1)S(1)}, bf16[3,4,16,896]{3,2,1,0:T(8,128)(2,1)S(1)}, u32[]{:S(2)}, u32[]{:S(2)}) collective-permute-start(bf16[3,4,16,896]{3,2,1,0:T(8,128)(2,1)S(1)} %get-tuple-element.69), channel_id=1, source_target_pairs={{0,128},{128,0},{1,129},{129,1},{2,130},{130,2},{3,131},{131,3},{4... | collective-permute-start | bytes 1032200 | tf_op jit(solution)/shard_map/ppermute | solution.py:24
  81.4 16.1 %collective-permute-start.19 = (bf16[256,2048]{1,0:T(8,128)(2,1)S(1)}, bf16[256,2048]{1,0:T(8,128)(2,1)S(1)}, u32[]{:S(2)}, u32[]{:S(2)}) collective-permute-start(bf16[256,2048]{1,0:T(8,128)(2,1)S(1)} %pad_maximum_fusion.1), channel_id=1, source_target_pairs={{0,96},{1,33},{32,64},{33,1},{64,32},{65,97},{96,0},{97,65},{2,98}... | collective-permute-start | bytes 3145736 | tf_op jit(solution)/shard_map/ppermute | solution.py:20
  97.5 14.8 %collective-permute-start.20 = (bf16[2,2,128,1024]{3,2,1,0:T(8,128)(2,1)S(1)}, bf16[2,2,128,1024]{3,2,1,0:T(8,128)(2,1)S(1)}, u32[]{:S(2)}, u32[]{:S(2)}) collective-permute-start(bf16[2,2,128,1024]{3,2,1,0:T(8,128)(2,1)S(1)} %get-tuple-element.39), channel_id=1, source_target_pairs={{0,32},{1,97},{32,0},{33,65},{64,96},{65,33},{96,64},{97,1},{2,34}... | collective-permute-start | bytes 3145736 | tf_op jit(solution)/shard_map/ppermute | solution.py:20
  97.5 7.3 %collective-permute-start.21 = (bf16[3,4,16,896]{3,2,1,0:T(8,128)(2,1)S(1)}, bf16[3,4,16,896]{3,2,1,0:T(8,128)(2,1)S(1)}, u32[]{:S(2)}, u32[]{:S(2)}) collective-permute-start(bf16[3,4,16,896]{3,2,1,0:T(8,128)(2,1)S(1)} %collective-permute-done.16), channel_id=1, source_target_pairs={{0,2},{1,7},{2,0},{3,5},{4,6},{5,3},{6,4},{7,1},{8,10},{9,15},{10,... | collective-permute-start | bytes 1032200 | tf_op jit(solution)/shard_map/ppermute | solution.py:20
  104.8 13.0 %collective-permute-start.23 = (bf16[2,3,4,16,896]{4,3,2,1,0:T(8,128)(2,1)S(1)}, bf16[2,3,4,16,896]{4,3,2,1,0:T(8,128)(2,1)S(1)}, u32[]{:S(2)}, u32[]{:S(2)}) collective-permute-start(bf16[2,3,4,16,896]{4,3,2,1,0:T(8,128)(2,1)S(1)} %pad_maximum_fusion.4.refs_3_), channel_id=1, source_target_pairs={{0,6},{1,3},{2,4},{3,1},{4,2},{5,7},{6,0},{7,5},{8,14},{9,11},{10,... | collective-permute-start | bytes 2064392 | tf_op jit(solution)/shard_map/ppermute | solution.py:20
  112.6 10.5 %collective-permute-start.22 = (bf16[2,128,1024]{2,1,0:T(8,128)(2,1)S(1)}, bf16[2,128,1024]{2,1,0:T(8,128)(2,1)S(1)}, u32[]{:S(2)}, u32[]{:S(2)}) collective-permute-start(bf16[2,128,1024]{2,1,0:T(8,128)(2,1)S(1)} %fusion.3), channel_id=1, source_target_pairs={{0,96},{1,33},{32,64},{33,1},{64,32},{65,97},{96,0},{97,65},{2,98}... | collective-permute-start | bytes 1572872 | tf_op jit(solution)/shard_map/ppermute | solution.py:20
  114.1 11.7 %collective-permute-start.25 = (bf16[2,3,4,16,896]{4,3,2,1,0:T(8,128)(2,1)S(1)}, bf16[2,3,4,16,896]{4,3,2,1,0:T(8,128)(2,1)S(1)}, u32[]{:S(2)}, u32[]{:S(2)}) collective-permute-start(bf16[2,3,4,16,896]{4,3,2,1,0:T(8,128)(2,1)S(1)} %pad_maximum_fusion.4.refs_3_), channel_id=1, source_target_pairs={{0,1},{1,0},{2,3},{3,2},{4,5},{5,4},{6,7},{7,6},{8,9},{9,8},{10,11... | collective-permute-start | bytes 2064392 | tf_op jit(solution)/shard_map/ppermute | solution.py:24
  117.8 7.9 %collective-permute-start.26 = (bf16[2,3,4,16,896]{4,3,2,1,0:T(8,128)(2,1)S(1)}, bf16[2,3,4,16,896]{4,3,2,1,0:T(8,128)(2,1)S(1)}, u32[]{:S(2)}, u32[]{:S(2)}) collective-permute-start(bf16[2,3,4,16,896]{4,3,2,1,0:T(8,128)(2,1)S(1)} %collective-permute-done.23.refs_4_), channel_id=1, source_target_pairs={{0,1},{1,0},{2,3},{3,2},{4,5},{5,4},{6,7},{7,6},{8,9},{9,8},{10,11... | collective-permute-start | bytes 2064392 | tf_op jit(solution)/shard_map/ppermute | solution.py:24
  124.4 8.4 %collective-permute-start.24 = (bf16[2,32,2048]{2,1,0:T(8,128)(2,1)S(1)}, bf16[2,32,2048]{2,1,0:T(8,128)(2,1)S(1)}, u32[]{:S(2)}, u32[]{:S(2)}) collective-permute-start(bf16[2,32,2048]{2,1,0:T(8,128)(2,1)S(1)} %pad_maximum_fusion.9), channel_id=1, source_target_pairs={{0,8},{1,25},{8,0},{9,17},{16,24},{17,9},{24,16},{25,1},{2,10},{3,... | collective-permute-start | bytes 786440 | tf_op jit(solution)/shard_map/ppermute | solution.py:20
  132.9 16.9 %collective-permute-start.27 = (bf16[32,2048]{1,0:T(8,128)(2,1)S(1)}, bf16[32,2048]{1,0:T(8,128)(2,1)S(1)}, u32[]{:S(2)}, u32[]{:S(2)}) collective-permute-start(bf16[32,2048]{1,0:T(8,128)(2,1)S(1)} %fusion.25), channel_id=1, source_target_pairs={{0,24},{1,9},{8,16},{9,1},{16,8},{17,25},{24,0},{25,17},{2,26},{3,... | collective-permute-start | bytes 393224 | tf_op jit(solution)/shard_map/ppermute | solution.py:20
  (8 other events, 81.9 us)
where the time goes:
time: 151 us; the launch traced here: 150 us
  waiting for transfers between devices  78.6 us (52%)
  starting transfers between devices  44.3 us (29%)
  Pallas kernels  19.4 us (13%)
  other arithmetic  3.79 us (3%)
  matrix products  2.32 us (2%)
    ppermute x20, waiting for transfers between devices, exchange(): return lax.ppermute(value, (axis, 'core'), pairs)  70.2 us
    ppermute x20, starting transfers between devices, exchange(): return lax.ppermute(value, (axis, 'core'), pairs)  39.8 us
    pallas_call x5, Pallas kernels, call(): pl.pallas_call(kernel, in_specs=[scalars(), scalars(), *(vmem for _ in op...  19.4 us
    ppermute x8, waiting for transfers between devices, swap(): return lax.ppermute(value, axis, [(0, 1), (1, 0)])  8.46 us
    ppermute x8, starting transfers between devices, swap(): return lax.ppermute(value, axis, [(0, 1), (1, 0)])  4.53 us
  transfers between devices with their start and end apart: 28, of which 20 were waited for; matrix products, arithmetic and copies ran while one was open for 4% of the time, Pallas kernels for 13%

commit v1 on v0

--- a/solution.py
+++ b/solution.py
@@ -49,17 +49,15 @@
     )
 
 
-def call(kernel, outs, operands, flops, scratch=(), **grid):
+def call(kernel, outs, operands):
     vmem = pl.BlockSpec(memory_space=pltpu.VMEM)
     return pl.pallas_call(
         kernel,
         in_specs=[scalars(), scalars(), *(vmem for _ in operands[2:])],
-        out_specs=grid.pop("out_specs", [vmem] * len(outs)),
+        out_specs=[vmem] * len(outs),
         out_shape=outs,
-        scratch_shapes=list(scratch),
         compiler_params=pltpu.CompilerParams(vmem_limit_bytes=30 << 20),
-        cost_estimate=pl.CostEstimate(flops=flops, bytes_accessed=1 << 20, transcendentals=0),
-        **grid,
+        cost_estimate=pl.CostEstimate(flops=1 << 20, bytes_accessed=1 << 10, transcendentals=0),
     )(*operands)
 
 
@@ -110,7 +108,7 @@
     tok, feats = 4 * pieces[0].shape[0], pieces[0].shape[1]
     sides = len(weights)
     shape = jax.ShapeDtypeStruct((4, sides, 4, tok // 32, hid), F32)
-    return call(kernel, [shape, shape], (core, mask, *pieces, *weights), 2 * sides * tok * feats * hid)
+    return call(kernel, [shape, shape], (core, mask, *pieces, *weights))
 
 
 def outputs_kernel(core, mask, two, rest, two_swapped, rest_swapped, wg, wu, wd, kept, sent):
@@ -141,7 +139,7 @@
     tok = 32 * acts[0].shape[3]
     shape = (2, 2, tok // 4, feats)
     outs = [jax.ShapeDtypeStruct(shape, F32), jax.ShapeDtypeStruct(shape, BF16)]
-    return call(outputs_kernel, outs, (core, mask, *acts, w_gate, w_up, w_down), 6 * tok * hid * feats)
+    return call(outputs_kernel, outs, (core, mask, *acts, w_gate, w_up, w_down))
 
 
 def own_grads_kernel(core, mask, *refs):
@@ -156,51 +154,37 @@
 
 
 def own_grads(core, mask, tokens, cots, acts):
-    feats, hid, count = tokens[0].shape[1], acts[0].shape[-1], 4 * tokens[0].shape[0]
+    feats, hid = tokens[0].shape[1], acts[0].shape[-1]
     outs = [
         jax.ShapeDtypeStruct((hid // BLK, feats, 2 * BLK), F32),
         jax.ShapeDtypeStruct((hid, feats), F32),
     ]
-    return call(own_grads_kernel, outs, (core, mask, *tokens, *cots, *acts), 6 * count * feats * hid)
+    return call(own_grads_kernel, outs, (core, mask, *tokens, *cots, *acts))
 
 
 def all_grads_kernel(core, mask, *refs):
     theirs, acts, own_both, own_down = refs[:3], refs[3:7], refs[7], refs[8]
-    grad_gate, grad_up, grad_down, tok_t, cot = refs[9:]
-    j = pl.program_id(0)
-    feats = tok_t.shape[0]
-
-    @pl.when(j == 0)
-    def _():
-        rows = jnp.concatenate(row_pieces(core[0] == 0, *theirs), axis=0)
-        tok_t[...] = rows[:, :feats].T
-        cot[...] = rows[:, feats:]
-
-    cols = pl.ds(pl.multiple_of(j * BLK, BLK), BLK)
-    hidden, gate, up = (acts_rows(side, *(ref.at[:, :, :, :, cols] for ref in acts)) for side in range(3))
-    both = jnp.dot(tok_t[...], jnp.concatenate([gate, up], axis=1), preferred_element_type=F32)
-    both = (both + own_both[j]).astype(BF16)
-    down = lax.dot_general(hidden, cot[...], COLS, preferred_element_type=F32)
-    down = (down + own_down[cols, :]).astype(BF16)
-    for k, spot in enumerate(blocks(feats // BLK)):
-        grad_gate[spot, :] = keep(mask[k, j], both[spot, :BLK])
-        grad_up[spot, :] = keep(mask[k, j], both[spot, BLK:])
-        grad_down[:, spot] = keep(mask[k, j], down[:, spot])
+    grad_gate, grad_up, grad_down = refs[9:]
+    feats = own_down.shape[1]
+    rows = jnp.concatenate(row_pieces(core[0] == 0, *theirs), axis=0)
+    tok_t, cot = rows[:, :feats].T, rows[:, feats:]
+    for j, cols in enumerate(blocks(acts[0].shape[-1] // BLK)):
+        hidden, gate, up = (acts_rows(side, *(ref.at[:, :, :, :, cols] for ref in acts)) for side in range(3))
+        both = jnp.dot(tok_t, jnp.concatenate([gate, up], axis=1), preferred_element_type=F32)
+        both = (both + own_both[j]).astype(BF16)
+        down = lax.dot_general(hidden, cot, COLS, preferred_element_type=F32)
+        down = (down + own_down[cols, :]).astype(BF16)
+        for k, spot in enumerate(blocks(feats // BLK)):
+            grad_gate[spot, cols] = keep(mask[k, j], both[spot, :BLK])
+            grad_up[spot, cols] = keep(mask[k, j], both[spot, BLK:])
+            grad_down[cols, spot] = keep(mask[k, j], down[:, spot])
 
 
 def all_grads(core, mask, theirs, acts, own):
-    feats, hid, count = theirs[0].shape[1] // 2, acts[0].shape[-1], 4 * theirs[0].shape[0]
+    feats, hid = theirs[0].shape[1] // 2, acts[0].shape[-1]
     up = jax.ShapeDtypeStruct((feats, hid), BF16)
-    up_tile = pl.BlockSpec((feats, BLK), lambda j: (0, j))
-    return call(
-        all_grads_kernel,
-        [up, up, jax.ShapeDtypeStruct((hid, feats), BF16)],
-        (core, mask, *theirs, *acts, *own),
-        6 * count * feats * hid,
-        [pltpu.VMEM((feats, count), BF16), pltpu.VMEM((count, feats), BF16)],
-        grid=(hid // BLK,),
-        out_specs=[up_tile, up_tile, pl.BlockSpec((BLK, feats), lambda j: (j, 0))],
-    )
+    outs = [up, up, jax.ShapeDtypeStruct((hid, feats), BF16)]
+    return call(all_grads_kernel, outs, (core, mask, *theirs, *acts, *own))
 
 
 def frame(rows):
@@ -276,8 +260,8 @@
     their_pair = jnp.stack([their_acts, exchange(after(their_acts, far), "x", 0)])
     own = own_grads(core, block_mask, tokens, cots, acts)
     their_far = exchange(their_pair, "x", 1)
-    both = kept + after(exchange(after(sent, their_rest), "y", 0)).astype(F32)
-    second = exchange(after(both[1].astype(BF16), their_pair), "y", 1)
+    both = kept + exchange(after(sent, their_rest), "y", 0).astype(F32)
+    second = exchange(after(both[1].astype(BF16), own[0], their_pair), "y", 1)
     total = both[0] + second.astype(F32)
 
     total = after(total, their_far)

time: 151 us -> 141 us (0.934)
  the two profiles are of different devices: /device:TPU:56 before, /device:TPU:1 now
where the time goes in v1:
time: 141 us
  waiting for transfers between devices  62.9 us (45%)
  starting transfers between devices  51.1 us (36%)
  Pallas kernels  18.7 us (13%)
  other arithmetic  3.95 us (3%)
  matrix products  2.31 us (2%)
    ppermute x20, waiting for transfers between devices, exchange(): return lax.ppermute(value, (axis, 'core'), pairs)  59 us
    ppermute x20, starting transfers between devices, exchange(): return lax.ppermute(value, (axis, 'core'), pairs)  31.9 us
    ppermute x8, starting transfers between devices, swap(): return lax.ppermute(value, axis, [(0, 1), (1, 0)])  19.3 us
    pallas_call x5, Pallas kernels, call(): pl.pallas_call(kernel, in_specs=[scalars(), scalars(), *(vmem for _ in op...  18.7 us
    ppermute x8, waiting for transfers between devices, swap(): return lax.ppermute(value, axis, [(0, 1), (1, 0)])  3.88 us
  transfers between devices with their start and end apart: 28, of which 19 were waited for; matrix products, arithmetic and copies ran while one was open for 4% of the time, Pallas kernels for 13%

profile of v1, /device:TPU:1, one launch (start us, length us, event | category | flops | bytes accessed | tf_op | source)
XLA Modules:
  0.0 141.0 jit_solution(18435437316688531177)
XLA Ops:
  0.6 6.9 %collective-permute-start = (bf16[32,1024]{1,0:T(8,128)(2,1)}, bf16[32,1024]{1,0:T(8,128)(2,1)S(1)}, u32[]{:S(2)}, u32[]{:S(2)}) collective-permute-start(bf16[32,1024]{1,0:T(8,128)(2,1)} %param.7), channel_id=1, source_target_pairs={{0,8},{1,25},{8,0},{9,17},{16,24},{17,9},{24,16},{25,1},{2,10},{3,... | collective-permute-start | bytes 196616 | tf_op jit(solution)/shard_map/ppermute | solution.py:20
  10.4 3.5 %collective-permute-done.1 = bf16[32,1024]{1,0:T(8,128)(2,1)S(1)} collective-permute-done((bf16[32,1024]{1,0:T(8,128)(2,1)}, bf16[32,1024]{1,0:T(8,128)(2,1)S(1)}, u32[]{:S(2)}, u32[]{:S(2)}) %collective-permute-start.1) | collective-permute-done | bytes 65568 | tf_op jit(solution)/shard_map/ppermute | solution.py:20
  17.2 3.0 %collective-permute-done.2 = bf16[64,1024]{1,0:T(8,128)(2,1)S(1)} collective-permute-done((bf16[64,1024]{1,0:T(8,128)(2,1)S(1)}, bf16[64,1024]{1,0:T(8,128)(2,1)S(1)}, u32[]{:S(2)}, u32[]{:S(2)}) %collective-permute-start.2) | collective-permute-done | bytes 131104 | tf_op jit(solution)/shard_map/ppermute | solution.py:20
  24.2 2.8 %collective-permute-start.6 = (bf16[128,1024]{1,0:T(8,128)(2,1)S(1)}, bf16[128,1024]{1,0:T(8,128)(2,1)S(1)}, u32[]{:S(2)}, u32[]{:S(2)}) collective-permute-start(bf16[128,1024]{1,0:T(8,128)(2,1)S(1)} %convolution_convert_fusion.own.refs_3_), channel_id=1, source_target_pairs={{0,32},{1,97},{32,0},{33,65},{64,96},{65,33},{96,64},{97,1},{2,34}... | collective-permute-start | bytes 786440 | tf_op jit(solution)/shard_map/ppermute | solution.py:20
  27.8 3.0 %collective-permute-done.6.near.refs_4_ = bf16[128,1024]{1,0:T(8,128)(2,1)S(1)} collective-permute-done((bf16[128,1024]{1,0:T(8,128)(2,1)S(1)}, bf16[128,1024]{1,0:T(8,128)(2,1)S(1)}, u32[]{:S(2)}, u32[]{:S(2)}) %collective-permute-start.6) | collective-permute-done | bytes 262176 | tf_op jit(solution)/shard_map/ppermute | solution.py:20
  31.3 6.4 %collective-permute-done.5.rest.refs_2_ = bf16[256,1024]{1,0:T(8,128)(2,1)S(1)} collective-permute-done((bf16[256,1024]{1,0:T(8,128)(2,1)S(1)}, bf16[256,1024]{1,0:T(8,128)(2,1)S(1)}, u32[]{:S(2)}, u32[]{:S(2)}) %collective-permute-start.5) | collective-permute-done | bytes 524320 | tf_op jit(solution)/shard_map/ppermute | solution.py:20
  37.7 2.7 %shard_map.110 = (f32[4,2,4,16,896]{4,3,2,1,0:T(8,128)S(1)}, f32[4,2,4,16,896]{4,3,2,1,0:T(8,128)S(1)}) custom-call(s32[1]{0:T(128)} %bitcast.2.core, s32[8,7]{1,0:T(8,128)S(1)} %copy-done.3, bf16[128,1024]{1,0:T(8,128)(2,1)S(1)} %convolution_convert_fusion.1.own.refs_0_, bf16[128,1024]{1,0:T(8,128)(2,1)S(1)} %collective-permute-done.3.near.refs_1_, ...), custom_call_target="tpu_custom_call" | custom-call | flops 1048576 | bytes 1024 | tf_op jit(solution)/shard_map/pallas_call | solution.py:54
  40.9 2.4 %collective-permute-done.8.rest.refs_5_ = bf16[256,1024]{1,0:T(8,128)(2,1)S(1)} collective-permute-done((bf16[256,1024]{1,0:T(8,128)(2,1)S(1)}, bf16[256,1024]{1,0:T(8,128)(2,1)S(1)}, u32[]{:S(2)}, u32[]{:S(2)}) %collective-permute-start.8) | collective-permute-done | bytes 524320 | tf_op jit(solution)/shard_map/ppermute | solution.py:20
  50.0 2.6 %collective-permute-start.11 = (bf16[2,3,4,16,896]{4,3,2,1,0:T(8,128)(2,1)S(1)}, bf16[2,3,4,16,896]{4,3,2,1,0:T(8,128)(2,1)S(1)}, u32[]{:S(2)}, u32[]{:S(2)}) collective-permute-start(bf16[2,3,4,16,896]{4,3,2,1,0:T(8,128)(2,1)S(1)} %pad_maximum_fusion.2), channel_id=1, source_target_pairs={{0,2},{1,7},{2,0},{3,5},{4,6},{5,3},{6,4},{7,1},{8,10},{9,15},{10,... | collective-permute-start | bytes 2064392 | tf_op jit(solution)/shard_map/ppermute | solution.py:20
  52.6 3.0 %collective-permute-start.12 = (bf16[128,2048]{1,0:T(8,128)(2,1)S(1)}, bf16[128,2048]{1,0:T(8,128)(2,1)S(1)}, u32[]{:S(2)}, u32[]{:S(2)}) collective-permute-start(bf16[128,2048]{1,0:T(8,128)(2,1)S(1)} %collective-permute-done.9.refs_0_), channel_id=1, source_target_pairs={{0,32},{1,97},{32,0},{33,65},{64,96},{65,33},{96,64},{97,1},{2,34}... | collective-permute-start | bytes 1572872 | tf_op jit(solution)/shard_map/ppermute | solution.py:20
  55.7 5.3 %collective-permute-done.11 = bf16[2,3,4,16,896]{4,3,2,1,0:T(8,128)(2,1)S(1)} collective-permute-done((bf16[2,3,4,16,896]{4,3,2,1,0:T(8,128)(2,1)S(1)}, bf16[2,3,4,16,896]{4,3,2,1,0:T(8,128)(2,1)S(1)}, u32[]{:S(2)}, u32[]{:S(2)}) %collective-permute-start.11) | collective-permute-done | bytes 688160 | tf_op jit(solution)/shard_map/ppermute | solution.py:20
  62.1 6.4 %collective-permute-done.13 = bf16[3,4,16,896]{3,2,1,0:T(8,128)(2,1)S(1)} collective-permute-done((bf16[3,4,16,896]{3,2,1,0:T(8,128)(2,1)S(1)}, bf16[3,4,16,896]{3,2,1,0:T(8,128)(2,1)S(1)}, u32[]{:S(2)}, u32[]{:S(2)}) %collective-permute-start.13) | collective-permute-done | bytes 344096 | tf_op jit(solution)/shard_map/ppermute | solution.py:20
  70.8 5.4 %collective-permute-done.14 = bf16[3,4,16,896]{3,2,1,0:T(8,128)(2,1)S(1)} collective-permute-done((bf16[3,4,16,896]{3,2,1,0:T(8,128)(2,1)S(1)}, bf16[3,4,16,896]{3,2,1,0:T(8,128)(2,1)S(1)}, u32[]{:S(2)}, u32[]{:S(2)}) %collective-permute-start.14) | collective-permute-done | bytes 344096 | tf_op jit(solution)/shard_map/ppermute | solution.py:20
  76.6 7.6 %collective-permute-start.17 = (bf16[2,3,4,16,896]{4,3,2,1,0:T(8,128)(2,1)S(1)}, bf16[2,3,4,16,896]{4,3,2,1,0:T(8,128)(2,1)S(1)}, u32[]{:S(2)}, u32[]{:S(2)}) collective-permute-start(bf16[2,3,4,16,896]{4,3,2,1,0:T(8,128)(2,1)S(1)} %pad_maximum_fusion.3.two.refs_6_), channel_id=1, source_target_pairs={{0,1},{1,0},{2,3},{3,2},{4,5},{5,4},{6,7},{7,6},{8,9},{9,8},{10,11... | collective-permute-start | bytes 2064392 | tf_op jit(solution)/shard_map/ppermute | solution.py:24
  86.4 5.1 %collective-permute-start.18 = (bf16[2,3,4,16,896]{4,3,2,1,0:T(8,128)(2,1)S(1)}, bf16[2,3,4,16,896]{4,3,2,1,0:T(8,128)(2,1)S(1)}, u32[]{:S(2)}, u32[]{:S(2)}) collective-permute-start(bf16[2,3,4,16,896]{4,3,2,1,0:T(8,128)(2,1)S(1)} %collective-permute-done.15.rest.refs_7_), channel_id=1, source_target_pairs={{0,1},{1,0},{2,3},{3,2},{4,5},{5,4},{6,7},{7,6},{8,9},{9,8},{10,11... | collective-permute-start | bytes 2064392 | tf_op jit(solution)/shard_map/ppermute | solution.py:24
  93.3 4.0 %shard_map.112 = (f32[2,2,128,1024]{3,2,1,0:T(8,128)S(1)}, bf16[2,2,128,1024]{3,2,1,0:T(8,128)(2,1)S(1)}) custom-call(s32[1]{0:T(128)} %bitcast.2.core, s32[8,7]{1,0:T(8,128)S(1)} %copy-done.3, bf16[2,3,4,16,896]{4,3,2,1,0:T(8,128)(2,1)S(1)} %pad_maximum_fusion.3.two.refs_6_, bf16[2,3,4,16,896]{4,3,2,1,0:T(8,128)(2,1)S(1)} %collective-permute-done.15.rest.refs_7_, ...), custom_call_target="tpu_custom_call" | custom-call | flops 1048576 | bytes 1024 | tf_op jit(solution)/shard_map/pallas_call | solution.py:54
  99.1 2.5 %collective-permute-start.21 = (bf16[3,4,16,896]{3,2,1,0:T(8,128)(2,1)S(1)}, bf16[3,4,16,896]{3,2,1,0:T(8,128)(2,1)S(1)}, u32[]{:S(2)}, u32[]{:S(2)}) collective-permute-start(bf16[3,4,16,896]{3,2,1,0:T(8,128)(2,1)S(1)} %collective-permute-done.16), channel_id=1, source_target_pairs={{0,2},{1,7},{2,0},{3,5},{4,6},{5,3},{6,4},{7,1},{8,10},{9,15},{10,... | collective-permute-start | bytes 1032200 | tf_op jit(solution)/shard_map/ppermute | solution.py:20
  101.6 4.8 %collective-permute-done.21 = bf16[3,4,16,896]{3,2,1,0:T(8,128)(2,1)S(1)} collective-permute-done((bf16[3,4,16,896]{3,2,1,0:T(8,128)(2,1)S(1)}, bf16[3,4,16,896]{3,2,1,0:T(8,128)(2,1)S(1)}, u32[]{:S(2)}, u32[]{:S(2)}) %collective-permute-start.21) | collective-permute-done | bytes 344096 | tf_op jit(solution)/shard_map/ppermute | solution.py:20
  106.6 3.8 %shard_map.113 = (f32[7,1024,256]{2,1,0:T(8,128)S(1)}, f32[896,1024]{1,0:T(8,128)S(1)}) custom-call(s32[1]{0:T(128)} %bitcast.2.core, s32[8,7]{1,0:T(8,128)S(1)} %copy-done.3, bf16[128,1024]{1,0:T(8,128)(2,1)S(1)} %convolution_convert_fusion.1.own.refs_0_, bf16[128,1024]{1,0:T(8,128)(2,1)S(1)} %collective-permute-done.3.near.refs_1_, ...), custom_call_target="tpu_custom_call" | custom-call | flops 1048576 | bytes 1024 | tf_op jit(solution)/shard_map/pallas_call | solution.py:54
  113.5 2.5 %collective-permute-start.25 = (bf16[2,3,4,16,896]{4,3,2,1,0:T(8,128)(2,1)S(1)}, bf16[2,3,4,16,896]{4,3,2,1,0:T(8,128)(2,1)S(1)}, u32[]{:S(2)}, u32[]{:S(2)}) collective-permute-start(bf16[2,3,4,16,896]{4,3,2,1,0:T(8,128)(2,1)S(1)} %pad_maximum_fusion.4.refs_3_), channel_id=1, source_target_pairs={{0,1},{1,0},{2,3},{3,2},{4,5},{5,4},{6,7},{7,6},{8,9},{9,8},{10,11... | collective-permute-start | bytes 2064392 | tf_op jit(solution)/shard_map/ppermute | solution.py:24
  117.5 4.3 %collective-permute-done.22 = bf16[2,128,1024]{2,1,0:T(8,128)(2,1)S(1)} collective-permute-done((bf16[2,128,1024]{2,1,0:T(8,128)(2,1)S(1)}, bf16[2,128,1024]{2,1,0:T(8,128)(2,1)S(1)}, u32[]{:S(2)}, u32[]{:S(2)}) %collective-permute-start.22) | collective-permute-done | bytes 524320 | tf_op jit(solution)/shard_map/ppermute | solution.py:20
  123.0 4.9 %collective-permute-start.24 = (bf16[2,32,2048]{2,1,0:T(8,128)(2,1)S(1)}, bf16[2,32,2048]{2,1,0:T(8,128)(2,1)S(1)}, u32[]{:S(2)}, u32[]{:S(2)}) collective-permute-start(bf16[2,32,2048]{2,1,0:T(8,128)(2,1)S(1)} %pad_maximum_fusion.9), channel_id=1, source_target_pairs={{0,8},{1,25},{8,0},{9,17},{16,24},{17,9},{24,16},{25,1},{2,10},{3,... | collective-permute-start | bytes 786440 | tf_op jit(solution)/shard_map/ppermute | solution.py:20
  127.9 6.3 %shard_map.114 = (bf16[1024,896]{1,0:T(8,128)(2,1)}, bf16[1024,896]{1,0:T(8,128)(2,1)}, bf16[896,1024]{1,0:T(8,128)(2,1)}) custom-call(s32[1]{0:T(128)} %bitcast.2.core, s32[8,7]{1,0:T(8,128)S(1)} %copy-done.3, bf16[128,2048]{1,0:T(8,128)(2,1)S(1)} %collective-permute-done.9.refs_0_, bf16[128,2048]{1,0:T(8,128)(2,1)S(1)} %collective-permute-done.12.refs_1_, ...), custom_call_target="tpu_custom_call" | custom-call | flops 1048576 | bytes 1024 | tf_op jit(solution)/shard_map/pallas_call | solution.py:54
  134.5 5.8 %collective-permute-done.27 = bf16[32,2048]{1,0:T(8,128)(2,1)S(1)} collective-permute-done((bf16[32,2048]{1,0:T(8,128)(2,1)S(1)}, bf16[32,2048]{1,0:T(8,128)(2,1)S(1)}, u32[]{:S(2)}, u32[]{:S(2)}) %collective-permute-start.27) | collective-permute-done | bytes 131104 | tf_op jit(solution)/shard_map/ppermute | solution.py:20
  (83 shorter events, 35.0 us)
Async XLA Ops:
  0.6 8.9 %collective-permute-start = (bf16[32,1024]{1,0:T(8,128)(2,1)}, bf16[32,1024]{1,0:T(8,128)(2,1)S(1)}, u32[]{:S(2)}, u32[]{:S(2)}) collective-permute-start(bf16[32,1024]{1,0:T(8,128)(2,1)} %param.7), channel_id=1, source_target_pairs={{0,8},{1,25},{8,0},{9,17},{16,24},{17,9},{24,16},{25,1},{2,10},{3,... | collective-permute-start | bytes 196616 | tf_op jit(solution)/shard_map/ppermute | solution.py:20
  15.6 7.6 %collective-permute-start.4 = (bf16[64,1024]{1,0:T(8,128)(2,1)S(1)}, bf16[64,1024]{1,0:T(8,128)(2,1)S(1)}, u32[]{:S(2)}, u32[]{:S(2)}) collective-permute-start(bf16[64,1024]{1,0:T(8,128)(2,1)S(1)} %pad_maximum_fusion.11), channel_id=1, source_target_pairs={{0,24},{1,9},{8,16},{9,1},{16,8},{17,25},{24,0},{25,17},{2,26},{3,... | collective-permute-start | bytes 393224 | tf_op jit(solution)/shard_map/ppermute | solution.py:20
  20.5 6.6 %collective-permute-start.3 = (bf16[128,1024]{1,0:T(8,128)(2,1)S(1)}, bf16[128,1024]{1,0:T(8,128)(2,1)S(1)}, u32[]{:S(2)}, u32[]{:S(2)}) collective-permute-start(bf16[128,1024]{1,0:T(8,128)(2,1)S(1)} %convolution_convert_fusion.1.own.refs_0_), channel_id=1, source_target_pairs={{0,32},{1,97},{32,0},{33,65},{64,96},{65,33},{96,64},{97,1},{2,34}... | collective-permute-start | bytes 786440 | tf_op jit(solution)/shard_map/ppermute | solution.py:20
  24.2 6.6 %collective-permute-start.6 = (bf16[128,1024]{1,0:T(8,128)(2,1)S(1)}, bf16[128,1024]{1,0:T(8,128)(2,1)S(1)}, u32[]{:S(2)}, u32[]{:S(2)}) collective-permute-start(bf16[128,1024]{1,0:T(8,128)(2,1)S(1)} %convolution_convert_fusion.own.refs_3_), channel_id=1, source_target_pairs={{0,32},{1,97},{32,0},{33,65},{64,96},{65,33},{96,64},{97,1},{2,34}... | collective-permute-start | bytes 786440 | tf_op jit(solution)/shard_map/ppermute | solution.py:20
  27.1 10.6 %collective-permute-start.5 = (bf16[256,1024]{1,0:T(8,128)(2,1)S(1)}, bf16[256,1024]{1,0:T(8,128)(2,1)S(1)}, u32[]{:S(2)}, u32[]{:S(2)}) collective-permute-start(bf16[256,1024]{1,0:T(8,128)(2,1)S(1)} %pad_maximum_fusion.5), channel_id=1, source_target_pairs={{0,96},{1,33},{32,64},{33,1},{64,32},{65,97},{96,0},{97,65},{2,98}... | collective-permute-start | bytes 1572872 | tf_op jit(solution)/shard_map/ppermute | solution.py:20
  27.2 13.7 %collective-permute-start.9 = (bf16[128,2048]{1,0:T(8,128)(2,1)S(1)}, bf16[128,2048]{1,0:T(8,128)(2,1)S(1)}, u32[]{:S(2)}, u32[]{:S(2)}) collective-permute-start(bf16[128,2048]{1,0:T(8,128)(2,1)S(1)} %pad_maximum_fusion.7), channel_id=1, source_target_pairs={{0,128},{128,0},{1,129},{129,1},{2,130},{130,2},{3,131},{131,3},{4... | collective-permute-start | bytes 1572872 | tf_op jit(solution)/shard_map/ppermute | solution.py:24
  30.9 12.4 %collective-permute-start.8 = (bf16[256,1024]{1,0:T(8,128)(2,1)S(1)}, bf16[256,1024]{1,0:T(8,128)(2,1)S(1)}, u32[]{:S(2)}, u32[]{:S(2)}) collective-permute-start(bf16[256,1024]{1,0:T(8,128)(2,1)S(1)} %pad_maximum_fusion.6), channel_id=1, source_target_pairs={{0,96},{1,33},{32,64},{33,1},{64,32},{65,97},{96,0},{97,65},{2,98}... | collective-permute-start | bytes 1572872 | tf_op jit(solution)/shard_map/ppermute | solution.py:20
  40.4 9.1 %collective-permute-start.7 = (f32[4,2,4,16,896]{4,3,2,1,0:T(8,128)S(1)}, f32[4,2,4,16,896]{4,3,2,1,0:T(8,128)S(1)}, u32[]{:S(2)}, u32[]{:S(2)}) collective-permute-start(f32[4,2,4,16,896]{4,3,2,1,0:T(8,128)S(1)} %get-tuple-element.31), channel_id=1, source_target_pairs={{0,1},{1,0},{2,3},{3,2},{4,5},{5,4},{6,7},{7,6},{8,9},{9,8},{10,11... | collective-permute-start | bytes 5505032 | tf_op jit(solution)/shard_map/ppermute | solution.py:24
  50.0 11.1 %collective-permute-start.11 = (bf16[2,3,4,16,896]{4,3,2,1,0:T(8,128)(2,1)S(1)}, bf16[2,3,4,16,896]{4,3,2,1,0:T(8,128)(2,1)S(1)}, u32[]{:S(2)}, u32[]{:S(2)}) collective-permute-start(bf16[2,3,4,16,896]{4,3,2,1,0:T(8,128)(2,1)S(1)} %pad_maximum_fusion.2), channel_id=1, source_target_pairs={{0,2},{1,7},{2,0},{3,5},{4,6},{5,3},{6,4},{7,1},{8,10},{9,15},{10,... | collective-permute-start | bytes 2064392 | tf_op jit(solution)/shard_map/ppermute | solution.py:20
  52.6 9.5 %collective-permute-start.12 = (bf16[128,2048]{1,0:T(8,128)(2,1)S(1)}, bf16[128,2048]{1,0:T(8,128)(2,1)S(1)}, u32[]{:S(2)}, u32[]{:S(2)}) collective-permute-start(bf16[128,2048]{1,0:T(8,128)(2,1)S(1)} %collective-permute-done.9.refs_0_), channel_id=1, source_target_pairs={{0,32},{1,97},{32,0},{33,65},{64,96},{65,33},{96,64},{97,1},{2,34}... | collective-permute-start | bytes 1572872 | tf_op jit(solution)/shard_map/ppermute | solution.py:20
  62.1 6.4 %collective-permute-start.13 = (bf16[3,4,16,896]{3,2,1,0:T(8,128)(2,1)S(1)}, bf16[3,4,16,896]{3,2,1,0:T(8,128)(2,1)S(1)}, u32[]{:S(2)}, u32[]{:S(2)}) collective-permute-start(bf16[3,4,16,896]{3,2,1,0:T(8,128)(2,1)S(1)} %fusion.10), channel_id=1, source_target_pairs={{0,6},{1,3},{2,4},{3,1},{4,2},{5,7},{6,0},{7,5},{8,14},{9,11},{10,... | collective-permute-start | bytes 1032200 | tf_op jit(solution)/shard_map/ppermute | solution.py:20
  68.8 7.4 %collective-permute-start.14 = (bf16[3,4,16,896]{3,2,1,0:T(8,128)(2,1)S(1)}, bf16[3,4,16,896]{3,2,1,0:T(8,128)(2,1)S(1)}, u32[]{:S(2)}, u32[]{:S(2)}) collective-permute-start(bf16[3,4,16,896]{3,2,1,0:T(8,128)(2,1)S(1)} %get-tuple-element.69), channel_id=1, source_target_pairs={{0,2},{1,7},{2,0},{3,5},{4,6},{5,3},{6,4},{7,1},{8,10},{9,15},{10,... | collective-permute-start | bytes 1032200 | tf_op jit(solution)/shard_map/ppermute | solution.py:20
  76.2 10.2 %collective-permute-start.15 = (bf16[2,3,4,16,896]{4,3,2,1,0:T(8,128)(2,1)S(1)}, bf16[2,3,4,16,896]{4,3,2,1,0:T(8,128)(2,1)S(1)}, u32[]{:S(2)}, u32[]{:S(2)}) collective-permute-start(bf16[2,3,4,16,896]{4,3,2,1,0:T(8,128)(2,1)S(1)} %pad_maximum_fusion.3.two.refs_6_), channel_id=1, source_target_pairs={{0,6},{1,3},{2,4},{3,1},{4,2},{5,7},{6,0},{7,5},{8,14},{9,11},{10,... | collective-permute-start | bytes 2064392 | tf_op jit(solution)/shard_map/ppermute | solution.py:20
  76.4 20.9 %collective-permute-start.19 = (bf16[256,2048]{1,0:T(8,128)(2,1)S(1)}, bf16[256,2048]{1,0:T(8,128)(2,1)S(1)}, u32[]{:S(2)}, u32[]{:S(2)}) collective-permute-start(bf16[256,2048]{1,0:T(8,128)(2,1)S(1)} %pad_maximum_fusion.1), channel_id=1, source_target_pairs={{0,96},{1,33},{32,64},{33,1},{64,32},{65,97},{96,0},{97,65},{2,98}... | collective-permute-start | bytes 3145736 | tf_op jit(solution)/shard_map/ppermute | solution.py:20
  76.5 7.8 %collective-permute-start.16 = (bf16[3,4,16,896]{3,2,1,0:T(8,128)(2,1)S(1)}, bf16[3,4,16,896]{3,2,1,0:T(8,128)(2,1)S(1)}, u32[]{:S(2)}, u32[]{:S(2)}) collective-permute-start(bf16[3,4,16,896]{3,2,1,0:T(8,128)(2,1)S(1)} %get-tuple-element.69), channel_id=1, source_target_pairs={{0,128},{128,0},{1,129},{129,1},{2,130},{130,2},{3,131},{131,3},{4... | collective-permute-start | bytes 1032200 | tf_op jit(solution)/shard_map/ppermute | solution.py:24
  76.6 14.9 %collective-permute-start.17 = (bf16[2,3,4,16,896]{4,3,2,1,0:T(8,128)(2,1)S(1)}, bf16[2,3,4,16,896]{4,3,2,1,0:T(8,128)(2,1)S(1)}, u32[]{:S(2)}, u32[]{:S(2)}) collective-permute-start(bf16[2,3,4,16,896]{4,3,2,1,0:T(8,128)(2,1)S(1)} %pad_maximum_fusion.3.two.refs_6_), channel_id=1, source_target_pairs={{0,1},{1,0},{2,3},{3,2},{4,5},{5,4},{6,7},{7,6},{8,9},{9,8},{10,11... | collective-permute-start | bytes 2064392 | tf_op jit(solution)/shard_map/ppermute | solution.py:24
  86.4 6.9 %collective-permute-start.18 = (bf16[2,3,4,16,896]{4,3,2,1,0:T(8,128)(2,1)S(1)}, bf16[2,3,4,16,896]{4,3,2,1,0:T(8,128)(2,1)S(1)}, u32[]{:S(2)}, u32[]{:S(2)}) collective-permute-start(bf16[2,3,4,16,896]{4,3,2,1,0:T(8,128)(2,1)S(1)} %collective-permute-done.15.rest.refs_7_), channel_id=1, source_target_pairs={{0,1},{1,0},{2,3},{3,2},{4,5},{5,4},{6,7},{7,6},{8,9},{9,8},{10,11... | collective-permute-start | bytes 2064392 | tf_op jit(solution)/shard_map/ppermute | solution.py:24
  97.4 15.2 %collective-permute-start.20 = (bf16[2,2,128,1024]{3,2,1,0:T(8,128)(2,1)S(1)}, bf16[2,2,128,1024]{3,2,1,0:T(8,128)(2,1)S(1)}, u32[]{:S(2)}, u32[]{:S(2)}) collective-permute-start(bf16[2,2,128,1024]{3,2,1,0:T(8,128)(2,1)S(1)} %get-tuple-element.39), channel_id=1, source_target_pairs={{0,32},{1,97},{32,0},{33,65},{64,96},{65,33},{96,64},{97,1},{2,34}... | collective-permute-start | bytes 3145736 | tf_op jit(solution)/shard_map/ppermute | solution.py:20
  99.1 7.3 %collective-permute-start.21 = (bf16[3,4,16,896]{3,2,1,0:T(8,128)(2,1)S(1)}, bf16[3,4,16,896]{3,2,1,0:T(8,128)(2,1)S(1)}, u32[]{:S(2)}, u32[]{:S(2)}) collective-permute-start(bf16[3,4,16,896]{3,2,1,0:T(8,128)(2,1)S(1)} %collective-permute-done.16), channel_id=1, source_target_pairs={{0,2},{1,7},{2,0},{3,5},{4,6},{5,3},{6,4},{7,1},{8,10},{9,15},{10,... | collective-permute-start | bytes 1032200 | tf_op jit(solution)/shard_map/ppermute | solution.py:20
  106.5 10.2 %collective-permute-start.23 = (bf16[2,3,4,16,896]{4,3,2,1,0:T(8,128)(2,1)S(1)}, bf16[2,3,4,16,896]{4,3,2,1,0:T(8,128)(2,1)S(1)}, u32[]{:S(2)}, u32[]{:S(2)}) collective-permute-start(bf16[2,3,4,16,896]{4,3,2,1,0:T(8,128)(2,1)S(1)} %pad_maximum_fusion.4.refs_3_), channel_id=1, source_target_pairs={{0,6},{1,3},{2,4},{3,1},{4,2},{5,7},{6,0},{7,5},{8,14},{9,11},{10,... | collective-permute-start | bytes 2064392 | tf_op jit(solution)/shard_map/ppermute | solution.py:20
  113.1 8.6 %collective-permute-start.22 = (bf16[2,128,1024]{2,1,0:T(8,128)(2,1)S(1)}, bf16[2,128,1024]{2,1,0:T(8,128)(2,1)S(1)}, u32[]{:S(2)}, u32[]{:S(2)}) collective-permute-start(bf16[2,128,1024]{2,1,0:T(8,128)(2,1)S(1)} %fusion.3), channel_id=1, source_target_pairs={{0,96},{1,33},{32,64},{33,1},{64,32},{65,97},{96,0},{97,65},{2,98}... | collective-permute-start | bytes 1572872 | tf_op jit(solution)/shard_map/ppermute | solution.py:20
  113.5 14.5 %collective-permute-start.25 = (bf16[2,3,4,16,896]{4,3,2,1,0:T(8,128)(2,1)S(1)}, bf16[2,3,4,16,896]{4,3,2,1,0:T(8,128)(2,1)S(1)}, u32[]{:S(2)}, u32[]{:S(2)}) collective-permute-start(bf16[2,3,4,16,896]{4,3,2,1,0:T(8,128)(2,1)S(1)} %pad_maximum_fusion.4.refs_3_), channel_id=1, source_target_pairs={{0,1},{1,0},{2,3},{3,2},{4,5},{5,4},{6,7},{7,6},{8,9},{9,8},{10,11... | collective-permute-start | bytes 2064392 | tf_op jit(solution)/shard_map/ppermute | solution.py:24
  116.7 11.3 %collective-permute-start.26 = (bf16[2,3,4,16,896]{4,3,2,1,0:T(8,128)(2,1)S(1)}, bf16[2,3,4,16,896]{4,3,2,1,0:T(8,128)(2,1)S(1)}, u32[]{:S(2)}, u32[]{:S(2)}) collective-permute-start(bf16[2,3,4,16,896]{4,3,2,1,0:T(8,128)(2,1)S(1)} %collective-permute-done.23.refs_4_), channel_id=1, source_target_pairs={{0,1},{1,0},{2,3},{3,2},{4,5},{5,4},{6,7},{7,6},{8,9},{9,8},{10,11... | collective-permute-start | bytes 2064392 | tf_op jit(solution)/shard_map/ppermute | solution.py:24
  123.0 11.2 %collective-permute-start.24 = (bf16[2,32,2048]{2,1,0:T(8,128)(2,1)S(1)}, bf16[2,32,2048]{2,1,0:T(8,128)(2,1)S(1)}, u32[]{:S(2)}, u32[]{:S(2)}) collective-permute-start(bf16[2,32,2048]{2,1,0:T(8,128)(2,1)S(1)} %pad_maximum_fusion.9), channel_id=1, source_target_pairs={{0,8},{1,25},{8,0},{9,17},{16,24},{17,9},{24,16},{25,1},{2,10},{3,... | collective-permute-start | bytes 786440 | tf_op jit(solution)/shard_map/ppermute | solution.py:20
  (8 other events, 80.0 us)

commit v2 on v1

--- a/solution.py
+++ b/solution.py
@@ -17,6 +17,11 @@
 
 def exchange(value, axis, step):
     pairs = [(2 * i + c, 2 * (i ^ PARTNERS[c][step]) + c) for i in range(4) for c in range(2)]
+    return lax.ppermute(value, (axis, "core"), pairs)
+
+
+def across(value, axis):
+    pairs = [(2 * i + c, 2 * (i ^ 2) + c) for i in range(4) for c in range(2)]
     return lax.ppermute(value, (axis, "core"), pairs)
 
 
@@ -268,11 +273,16 @@
     total = jnp.concatenate(
         [lax.dot_general(pick, side, COLS, precision="highest", preferred_element_type=F32) for side in total], axis=1
     ).reshape(4, rows, 2 * feats)
-    kept, sent = jnp.stack([total[0], total[2]]), jnp.stack([total[1], total[3]]).astype(BF16)
     theirs = (their_z, their_near, their_rest)
     their_acts = (their_pair, their_far, swap(their_pair, "core"), swap(their_far, "core"))
     grads = all_grads(core, block_mask, theirs, their_acts, own)
-    total = scatter(kept, sent, "zh", grads[0]).astype(BF16)
+    sent = total[1:].astype(BF16)
+    total = total[0] + (
+        exchange(sent[0], "zh", 0).astype(F32)
+        + exchange(sent[1], "zh", 1).astype(F32)
+        + across(sent[2], "zh").astype(F32)
+    )
+    total = total.astype(BF16)
     return total[:, :feats], total[:, feats:], *grads
 
 

time: 141 us -> 142 us (level)
  starting transfers between devices: 51.1 us -> 53.1 us
    ppermute x0 -> x1, starting transfers between devices: none -> 2.5 us  [across(): return lax.ppermute(value, (axis, 'core'), pairs)]
  transfers between devices with their start and end apart: 28 -> 29, of which waited for: 19 -> 19; matrix products, arithmetic and copies ran while one was open for 4% -> 4% of each run, Pallas kernels for 13% -> 13%
where the time goes in v2:
time: 142 us
  waiting for transfers between devices  61.7 us (43%)
  starting transfers between devices  53.1 us (37%)
  Pallas kernels  18.7 us (13%)
  other arithmetic  3.87 us (3%)
  matrix products  2.31 us (2%)
    ppermute x20, waiting for transfers between devices, exchange(): return lax.ppermute(value, (axis, 'core'), pairs)  57.8 us
    ppermute x20, starting transfers between devices, exchange(): return lax.ppermute(value, (axis, 'core'), pairs)  31.3 us
    ppermute x8, starting transfers between devices, swap(): return lax.ppermute(value, axis, [(0, 1), (1, 0)])  19.3 us
    pallas_call x5, Pallas kernels, call(): pl.pallas_call(kernel, in_specs=[scalars(), scalars(), *(vmem for _ in op...  18.7 us
    ppermute x8, waiting for transfers between devices, swap(): return lax.ppermute(value, axis, [(0, 1), (1, 0)])  3.88 us
  transfers between devices with their start and end apart: 29, of which 19 were waited for; matrix products, arithmetic and copies ran while one was open for 4% of the time, Pallas kernels for 13%

profile of v2, /device:TPU:1, one launch (start us, length us, event | category | flops | bytes accessed | tf_op | source)
XLA Modules:
  0.0 141.7 jit_solution(2429295976012183090)
XLA Ops:
  0.6 6.9 %collective-permute-start = (bf16[32,1024]{1,0:T(8,128)(2,1)}, bf16[32,1024]{1,0:T(8,128)(2,1)S(1)}, u32[]{:S(2)}, u32[]{:S(2)}) collective-permute-start(bf16[32,1024]{1,0:T(8,128)(2,1)} %param.7), channel_id=1, source_target_pairs={{0,8},{1,25},{8,0},{9,17},{16,24},{17,9},{24,16},{25,1},{2,10},{3,... | collective-permute-start | bytes 196616 | tf_op jit(solution)/shard_map/ppermute | solution.py:20
  10.4 3.5 %collective-permute-done.1 = bf16[32,1024]{1,0:T(8,128)(2,1)S(1)} collective-permute-done((bf16[32,1024]{1,0:T(8,128)(2,1)}, bf16[32,1024]{1,0:T(8,128)(2,1)S(1)}, u32[]{:S(2)}, u32[]{:S(2)}) %collective-permute-start.1) | collective-permute-done | bytes 65568 | tf_op jit(solution)/shard_map/ppermute | solution.py:20
  17.2 3.0 %collective-permute-done.2 = bf16[64,1024]{1,0:T(8,128)(2,1)S(1)} collective-permute-done((bf16[64,1024]{1,0:T(8,128)(2,1)S(1)}, bf16[64,1024]{1,0:T(8,128)(2,1)S(1)}, u32[]{:S(2)}, u32[]{:S(2)}) %collective-permute-start.2) | collective-permute-done | bytes 131104 | tf_op jit(solution)/shard_map/ppermute | solution.py:20
  24.2 2.8 %collective-permute-start.6 = (bf16[128,1024]{1,0:T(8,128)(2,1)S(1)}, bf16[128,1024]{1,0:T(8,128)(2,1)S(1)}, u32[]{:S(2)}, u32[]{:S(2)}) collective-permute-start(bf16[128,1024]{1,0:T(8,128)(2,1)S(1)} %convolution_convert_fusion.own.refs_3_), channel_id=1, source_target_pairs={{0,32},{1,97},{32,0},{33,65},{64,96},{65,33},{96,64},{97,1},{2,34}... | collective-permute-start | bytes 786440 | tf_op jit(solution)/shard_map/ppermute | solution.py:20
  27.8 3.0 %collective-permute-done.6.near.refs_4_ = bf16[128,1024]{1,0:T(8,128)(2,1)S(1)} collective-permute-done((bf16[128,1024]{1,0:T(8,128)(2,1)S(1)}, bf16[128,1024]{1,0:T(8,128)(2,1)S(1)}, u32[]{:S(2)}, u32[]{:S(2)}) %collective-permute-start.6) | collective-permute-done | bytes 262176 | tf_op jit(solution)/shard_map/ppermute | solution.py:20
  31.3 6.4 %collective-permute-done.5.rest.refs_2_ = bf16[256,1024]{1,0:T(8,128)(2,1)S(1)} collective-permute-done((bf16[256,1024]{1,0:T(8,128)(2,1)S(1)}, bf16[256,1024]{1,0:T(8,128)(2,1)S(1)}, u32[]{:S(2)}, u32[]{:S(2)}) %collective-permute-start.5) | collective-permute-done | bytes 524320 | tf_op jit(solution)/shard_map/ppermute | solution.py:20
  37.7 2.7 %shard_map.110 = (f32[4,2,4,16,896]{4,3,2,1,0:T(8,128)S(1)}, f32[4,2,4,16,896]{4,3,2,1,0:T(8,128)S(1)}) custom-call(s32[1]{0:T(128)} %bitcast.2.core, s32[8,7]{1,0:T(8,128)S(1)} %copy-done.3, bf16[128,1024]{1,0:T(8,128)(2,1)S(1)} %convolution_convert_fusion.1.own.refs_0_, bf16[128,1024]{1,0:T(8,128)(2,1)S(1)} %collective-permute-done.3.near.refs_1_, ...), custom_call_target="tpu_custom_call" | custom-call | flops 1048576 | bytes 1024 | tf_op jit(solution)/shard_map/pallas_call | solution.py:59
  50.0 2.6 %collective-permute-start.11 = (bf16[2,3,4,16,896]{4,3,2,1,0:T(8,128)(2,1)S(1)}, bf16[2,3,4,16,896]{4,3,2,1,0:T(8,128)(2,1)S(1)}, u32[]{:S(2)}, u32[]{:S(2)}) collective-permute-start(bf16[2,3,4,16,896]{4,3,2,1,0:T(8,128)(2,1)S(1)} %pad_maximum_fusion.2), channel_id=1, source_target_pairs={{0,2},{1,7},{2,0},{3,5},{4,6},{5,3},{6,4},{7,1},{8,10},{9,15},{10,... | collective-permute-start | bytes 2064392 | tf_op jit(solution)/shard_map/ppermute | solution.py:20
  52.6 3.0 %collective-permute-start.12 = (bf16[128,2048]{1,0:T(8,128)(2,1)S(1)}, bf16[128,2048]{1,0:T(8,128)(2,1)S(1)}, u32[]{:S(2)}, u32[]{:S(2)}) collective-permute-start(bf16[128,2048]{1,0:T(8,128)(2,1)S(1)} %collective-permute-done.9.refs_0_), channel_id=1, source_target_pairs={{0,32},{1,97},{32,0},{33,65},{64,96},{65,33},{96,64},{97,1},{2,34}... | collective-permute-start | bytes 1572872 | tf_op jit(solution)/shard_map/ppermute | solution.py:20
  55.7 5.3 %collective-permute-done.11 = bf16[2,3,4,16,896]{4,3,2,1,0:T(8,128)(2,1)S(1)} collective-permute-done((bf16[2,3,4,16,896]{4,3,2,1,0:T(8,128)(2,1)S(1)}, bf16[2,3,4,16,896]{4,3,2,1,0:T(8,128)(2,1)S(1)}, u32[]{:S(2)}, u32[]{:S(2)}) %collective-permute-start.11) | collective-permute-done | bytes 688160 | tf_op jit(solution)/shard_map/ppermute | solution.py:20
  62.1 6.4 %collective-permute-done.13 = bf16[3,4,16,896]{3,2,1,0:T(8,128)(2,1)S(1)} collective-permute-done((bf16[3,4,16,896]{3,2,1,0:T(8,128)(2,1)S(1)}, bf16[3,4,16,896]{3,2,1,0:T(8,128)(2,1)S(1)}, u32[]{:S(2)}, u32[]{:S(2)}) %collective-permute-start.13) | collective-permute-done | bytes 344096 | tf_op jit(solution)/shard_map/ppermute | solution.py:20
  70.8 5.4 %collective-permute-done.14 = bf16[3,4,16,896]{3,2,1,0:T(8,128)(2,1)S(1)} collective-permute-done((bf16[3,4,16,896]{3,2,1,0:T(8,128)(2,1)S(1)}, bf16[3,4,16,896]{3,2,1,0:T(8,128)(2,1)S(1)}, u32[]{:S(2)}, u32[]{:S(2)}) %collective-permute-start.14) | collective-permute-done | bytes 344096 | tf_op jit(solution)/shard_map/ppermute | solution.py:20
  76.6 7.6 %collective-permute-start.17 = (bf16[2,3,4,16,896]{4,3,2,1,0:T(8,128)(2,1)S(1)}, bf16[2,3,4,16,896]{4,3,2,1,0:T(8,128)(2,1)S(1)}, u32[]{:S(2)}, u32[]{:S(2)}) collective-permute-start(bf16[2,3,4,16,896]{4,3,2,1,0:T(8,128)(2,1)S(1)} %pad_maximum_fusion.3.two.refs_6_), channel_id=1, source_target_pairs={{0,1},{1,0},{2,3},{3,2},{4,5},{5,4},{6,7},{7,6},{8,9},{9,8},{10,11... | collective-permute-start | bytes 2064392 | tf_op jit(solution)/shard_map/ppermute | solution.py:29
  86.4 5.1 %collective-permute-start.18 = (bf16[2,3,4,16,896]{4,3,2,1,0:T(8,128)(2,1)S(1)}, bf16[2,3,4,16,896]{4,3,2,1,0:T(8,128)(2,1)S(1)}, u32[]{:S(2)}, u32[]{:S(2)}) collective-permute-start(bf16[2,3,4,16,896]{4,3,2,1,0:T(8,128)(2,1)S(1)} %collective-permute-done.15.rest.refs_7_), channel_id=1, source_target_pairs={{0,1},{1,0},{2,3},{3,2},{4,5},{5,4},{6,7},{7,6},{8,9},{9,8},{10,11... | collective-permute-start | bytes 2064392 | tf_op jit(solution)/shard_map/ppermute | solution.py:29
  93.3 4.0 %shard_map.112 = (f32[2,2,128,1024]{3,2,1,0:T(8,128)S(1)}, bf16[2,2,128,1024]{3,2,1,0:T(8,128)(2,1)S(1)}) custom-call(s32[1]{0:T(128)} %bitcast.2.core, s32[8,7]{1,0:T(8,128)S(1)} %copy-done.3, bf16[2,3,4,16,896]{4,3,2,1,0:T(8,128)(2,1)S(1)} %pad_maximum_fusion.3.two.refs_6_, bf16[2,3,4,16,896]{4,3,2,1,0:T(8,128)(2,1)S(1)} %collective-permute-done.15.rest.refs_7_, ...), custom_call_target="tpu_custom_call" | custom-call | flops 1048576 | bytes 1024 | tf_op jit(solution)/shard_map/pallas_call | solution.py:59
  99.1 2.5 %collective-permute-start.21 = (bf16[3,4,16,896]{3,2,1,0:T(8,128)(2,1)S(1)}, bf16[3,4,16,896]{3,2,1,0:T(8,128)(2,1)S(1)}, u32[]{:S(2)}, u32[]{:S(2)}) collective-permute-start(bf16[3,4,16,896]{3,2,1,0:T(8,128)(2,1)S(1)} %collective-permute-done.16), channel_id=1, source_target_pairs={{0,2},{1,7},{2,0},{3,5},{4,6},{5,3},{6,4},{7,1},{8,10},{9,15},{10,... | collective-permute-start | bytes 1032200 | tf_op jit(solution)/shard_map/ppermute | solution.py:20
  101.6 4.8 %collective-permute-done.21 = bf16[3,4,16,896]{3,2,1,0:T(8,128)(2,1)S(1)} collective-permute-done((bf16[3,4,16,896]{3,2,1,0:T(8,128)(2,1)S(1)}, bf16[3,4,16,896]{3,2,1,0:T(8,128)(2,1)S(1)}, u32[]{:S(2)}, u32[]{:S(2)}) %collective-permute-start.21) | collective-permute-done | bytes 344096 | tf_op jit(solution)/shard_map/ppermute | solution.py:20
  106.6 3.8 %shard_map.113 = (f32[7,1024,256]{2,1,0:T(8,128)S(1)}, f32[896,1024]{1,0:T(8,128)S(1)}) custom-call(s32[1]{0:T(128)} %bitcast.2.core, s32[8,7]{1,0:T(8,128)S(1)} %copy-done.3, bf16[128,1024]{1,0:T(8,128)(2,1)S(1)} %convolution_convert_fusion.1.own.refs_0_, bf16[128,1024]{1,0:T(8,128)(2,1)S(1)} %collective-permute-done.3.near.refs_1_, ...), custom_call_target="tpu_custom_call" | custom-call | flops 1048576 | bytes 1024 | tf_op jit(solution)/shard_map/pallas_call | solution.py:59
  113.5 2.5 %collective-permute-start.27 = (bf16[2,3,4,16,896]{4,3,2,1,0:T(8,128)(2,1)S(1)}, bf16[2,3,4,16,896]{4,3,2,1,0:T(8,128)(2,1)S(1)}, u32[]{:S(2)}, u32[]{:S(2)}) collective-permute-start(bf16[2,3,4,16,896]{4,3,2,1,0:T(8,128)(2,1)S(1)} %pad_maximum_fusion.4.refs_3_), channel_id=1, source_target_pairs={{0,1},{1,0},{2,3},{3,2},{4,5},{5,4},{6,7},{7,6},{8,9},{9,8},{10,11... | collective-permute-start | bytes 2064392 | tf_op jit(solution)/shard_map/ppermute | solution.py:29
  117.5 4.3 %collective-permute-done.22 = bf16[2,128,1024]{2,1,0:T(8,128)(2,1)S(1)} collective-permute-done((bf16[2,128,1024]{2,1,0:T(8,128)(2,1)S(1)}, bf16[2,128,1024]{2,1,0:T(8,128)(2,1)S(1)}, u32[]{:S(2)}, u32[]{:S(2)}) %collective-permute-start.22) | collective-permute-done | bytes 524320 | tf_op jit(solution)/shard_map/ppermute | solution.py:20
  123.0 2.5 %collective-permute-start.26 = (bf16[32,2048]{1,0:T(8,128)(2,1)S(1)}, bf16[32,2048]{1,0:T(8,128)(2,1)S(1)}, u32[]{:S(2)}, u32[]{:S(2)}) collective-permute-start(bf16[32,2048]{1,0:T(8,128)(2,1)S(1)} %get-tuple-element.61), channel_id=1, source_target_pairs={{0,16},{1,17},{8,24},{9,25},{16,0},{17,1},{24,8},{25,9},{2,18},{3,... | collective-permute-start | bytes 393224 | tf_op jit(solution)/shard_map/ppermute | solution.py:25
  125.5 4.4 %collective-permute-start.25 = (bf16[32,2048]{1,0:T(8,128)(2,1)S(1)}, bf16[32,2048]{1,0:T(8,128)(2,1)S(1)}, u32[]{:S(2)}, u32[]{:S(2)}) collective-permute-start(bf16[32,2048]{1,0:T(8,128)(2,1)S(1)} %get-tuple-element.62), channel_id=1, source_target_pairs={{0,24},{1,9},{8,16},{9,1},{16,8},{17,25},{24,0},{25,17},{2,26},{3,... | collective-permute-start | bytes 393224 | tf_op jit(solution)/shard_map/ppermute | solution.py:20
  130.0 6.3 %shard_map.114 = (bf16[1024,896]{1,0:T(8,128)(2,1)}, bf16[1024,896]{1,0:T(8,128)(2,1)}, bf16[896,1024]{1,0:T(8,128)(2,1)}) custom-call(s32[1]{0:T(128)} %bitcast.2.core, s32[8,7]{1,0:T(8,128)S(1)} %copy-done.3, bf16[128,2048]{1,0:T(8,128)(2,1)S(1)} %collective-permute-done.9.refs_0_, bf16[128,2048]{1,0:T(8,128)(2,1)S(1)} %collective-permute-done.12.refs_1_, ...), custom_call_target="tpu_custom_call" | custom-call | flops 1048576 | bytes 1024 | tf_op jit(solution)/shard_map/pallas_call | solution.py:59
  136.3 4.7 %collective-permute-done.25 = bf16[32,2048]{1,0:T(8,128)(2,1)S(1)} collective-permute-done((bf16[32,2048]{1,0:T(8,128)(2,1)S(1)}, bf16[32,2048]{1,0:T(8,128)(2,1)S(1)}, u32[]{:S(2)}, u32[]{:S(2)}) %collective-permute-start.25) | collective-permute-done | bytes 131104 | tf_op jit(solution)/shard_map/ppermute | solution.py:20
  (81 shorter events, 37.2 us)
Async XLA Ops:
  0.6 8.9 %collective-permute-start = (bf16[32,1024]{1,0:T(8,128)(2,1)}, bf16[32,1024]{1,0:T(8,128)(2,1)S(1)}, u32[]{:S(2)}, u32[]{:S(2)}) collective-permute-start(bf16[32,1024]{1,0:T(8,128)(2,1)} %param.7), channel_id=1, source_target_pairs={{0,8},{1,25},{8,0},{9,17},{16,24},{17,9},{24,16},{25,1},{2,10},{3,... | collective-permute-start | bytes 196616 | tf_op jit(solution)/shard_map/ppermute | solution.py:20
  15.6 7.6 %collective-permute-start.4 = (bf16[64,1024]{1,0:T(8,128)(2,1)S(1)}, bf16[64,1024]{1,0:T(8,128)(2,1)S(1)}, u32[]{:S(2)}, u32[]{:S(2)}) collective-permute-start(bf16[64,1024]{1,0:T(8,128)(2,1)S(1)} %pad_maximum_fusion.10), channel_id=1, source_target_pairs={{0,24},{1,9},{8,16},{9,1},{16,8},{17,25},{24,0},{25,17},{2,26},{3,... | collective-permute-start | bytes 393224 | tf_op jit(solution)/shard_map/ppermute | solution.py:20
  24.2 6.6 %collective-permute-start.6 = (bf16[128,1024]{1,0:T(8,128)(2,1)S(1)}, bf16[128,1024]{1,0:T(8,128)(2,1)S(1)}, u32[]{:S(2)}, u32[]{:S(2)}) collective-permute-start(bf16[128,1024]{1,0:T(8,128)(2,1)S(1)} %convolution_convert_fusion.own.refs_3_), channel_id=1, source_target_pairs={{0,32},{1,97},{32,0},{33,65},{64,96},{65,33},{96,64},{97,1},{2,34}... | collective-permute-start | bytes 786440 | tf_op jit(solution)/shard_map/ppermute | solution.py:20
  27.1 10.6 %collective-permute-start.5 = (bf16[256,1024]{1,0:T(8,128)(2,1)S(1)}, bf16[256,1024]{1,0:T(8,128)(2,1)S(1)}, u32[]{:S(2)}, u32[]{:S(2)}) collective-permute-start(bf16[256,1024]{1,0:T(8,128)(2,1)S(1)} %pad_maximum_fusion.5), channel_id=1, source_target_pairs={{0,96},{1,33},{32,64},{33,1},{64,32},{65,97},{96,0},{97,65},{2,98}... | collective-permute-start | bytes 1572872 | tf_op jit(solution)/shard_map/ppermute | solution.py:20
  27.2 13.7 %collective-permute-start.9 = (bf16[128,2048]{1,0:T(8,128)(2,1)S(1)}, bf16[128,2048]{1,0:T(8,128)(2,1)S(1)}, u32[]{:S(2)}, u32[]{:S(2)}) collective-permute-start(bf16[128,2048]{1,0:T(8,128)(2,1)S(1)} %pad_maximum_fusion.7), channel_id=1, source_target_pairs={{0,128},{128,0},{1,129},{129,1},{2,130},{130,2},{3,131},{131,3},{4... | collective-permute-start | bytes 1572872 | tf_op jit(solution)/shard_map/ppermute | solution.py:29
  30.9 12.4 %collective-permute-start.8 = (bf16[256,1024]{1,0:T(8,128)(2,1)S(1)}, bf16[256,1024]{1,0:T(8,128)(2,1)S(1)}, u32[]{:S(2)}, u32[]{:S(2)}) collective-permute-start(bf16[256,1024]{1,0:T(8,128)(2,1)S(1)} %pad_maximum_fusion.6), channel_id=1, source_target_pairs={{0,96},{1,33},{32,64},{33,1},{64,32},{65,97},{96,0},{97,65},{2,98}... | collective-permute-start | bytes 1572872 | tf_op jit(solution)/shard_map/ppermute | solution.py:20
  40.4 9.1 %collective-permute-start.7 = (f32[4,2,4,16,896]{4,3,2,1,0:T(8,128)S(1)}, f32[4,2,4,16,896]{4,3,2,1,0:T(8,128)S(1)}, u32[]{:S(2)}, u32[]{:S(2)}) collective-permute-start(f32[4,2,4,16,896]{4,3,2,1,0:T(8,128)S(1)} %get-tuple-element.30), channel_id=1, source_target_pairs={{0,1},{1,0},{2,3},{3,2},{4,5},{5,4},{6,7},{7,6},{8,9},{9,8},{10,11... | collective-permute-start | bytes 5505032 | tf_op jit(solution)/shard_map/ppermute | solution.py:29
  50.0 11.1 %collective-permute-start.11 = (bf16[2,3,4,16,896]{4,3,2,1,0:T(8,128)(2,1)S(1)}, bf16[2,3,4,16,896]{4,3,2,1,0:T(8,128)(2,1)S(1)}, u32[]{:S(2)}, u32[]{:S(2)}) collective-permute-start(bf16[2,3,4,16,896]{4,3,2,1,0:T(8,128)(2,1)S(1)} %pad_maximum_fusion.2), channel_id=1, source_target_pairs={{0,2},{1,7},{2,0},{3,5},{4,6},{5,3},{6,4},{7,1},{8,10},{9,15},{10,... | collective-permute-start | bytes 2064392 | tf_op jit(solution)/shard_map/ppermute | solution.py:20
  52.6 9.5 %collective-permute-start.12 = (bf16[128,2048]{1,0:T(8,128)(2,1)S(1)}, bf16[128,2048]{1,0:T(8,128)(2,1)S(1)}, u32[]{:S(2)}, u32[]{:S(2)}) collective-permute-start(bf16[128,2048]{1,0:T(8,128)(2,1)S(1)} %collective-permute-done.9.refs_0_), channel_id=1, source_target_pairs={{0,32},{1,97},{32,0},{33,65},{64,96},{65,33},{96,64},{97,1},{2,34}... | collective-permute-start | bytes 1572872 | tf_op jit(solution)/shard_map/ppermute | solution.py:20
  68.8 7.4 %collective-permute-start.14 = (bf16[3,4,16,896]{3,2,1,0:T(8,128)(2,1)S(1)}, bf16[3,4,16,896]{3,2,1,0:T(8,128)(2,1)S(1)}, u32[]{:S(2)}, u32[]{:S(2)}) collective-permute-start(bf16[3,4,16,896]{3,2,1,0:T(8,128)(2,1)S(1)} %get-tuple-element.66), channel_id=1, source_target_pairs={{0,2},{1,7},{2,0},{3,5},{4,6},{5,3},{6,4},{7,1},{8,10},{9,15},{10,... | collective-permute-start | bytes 1032200 | tf_op jit(solution)/shard_map/ppermute | solution.py:20
  76.2 10.2 %collective-permute-start.15 = (bf16[2,3,4,16,896]{4,3,2,1,0:T(8,128)(2,1)S(1)}, bf16[2,3,4,16,896]{4,3,2,1,0:T(8,128)(2,1)S(1)}, u32[]{:S(2)}, u32[]{:S(2)}) collective-permute-start(bf16[2,3,4,16,896]{4,3,2,1,0:T(8,128)(2,1)S(1)} %pad_maximum_fusion.3.two.refs_6_), channel_id=1, source_target_pairs={{0,6},{1,3},{2,4},{3,1},{4,2},{5,7},{6,0},{7,5},{8,14},{9,11},{10,... | collective-permute-start | bytes 2064392 | tf_op jit(solution)/shard_map/ppermute | solution.py:20
  76.4 20.9 %collective-permute-start.19 = (bf16[256,2048]{1,0:T(8,128)(2,1)S(1)}, bf16[256,2048]{1,0:T(8,128)(2,1)S(1)}, u32[]{:S(2)}, u32[]{:S(2)}) collective-permute-start(bf16[256,2048]{1,0:T(8,128)(2,1)S(1)} %pad_maximum_fusion.1), channel_id=1, source_target_pairs={{0,96},{1,33},{32,64},{33,1},{64,32},{65,97},{96,0},{97,65},{2,98}... | collective-permute-start | bytes 3145736 | tf_op jit(solution)/shard_map/ppermute | solution.py:20
  76.5 7.8 %collective-permute-start.16 = (bf16[3,4,16,896]{3,2,1,0:T(8,128)(2,1)S(1)}, bf16[3,4,16,896]{3,2,1,0:T(8,128)(2,1)S(1)}, u32[]{:S(2)}, u32[]{:S(2)}) collective-permute-start(bf16[3,4,16,896]{3,2,1,0:T(8,128)(2,1)S(1)} %get-tuple-element.66), channel_id=1, source_target_pairs={{0,128},{128,0},{1,129},{129,1},{2,130},{130,2},{3,131},{131,3},{4... | collective-permute-start | bytes 1032200 | tf_op jit(solution)/shard_map/ppermute | solution.py:29
  76.6 14.9 %collective-permute-start.17 = (bf16[2,3,4,16,896]{4,3,2,1,0:T(8,128)(2,1)S(1)}, bf16[2,3,4,16,896]{4,3,2,1,0:T(8,128)(2,1)S(1)}, u32[]{:S(2)}, u32[]{:S(2)}) collective-permute-start(bf16[2,3,4,16,896]{4,3,2,1,0:T(8,128)(2,1)S(1)} %pad_maximum_fusion.3.two.refs_6_), channel_id=1, source_target_pairs={{0,1},{1,0},{2,3},{3,2},{4,5},{5,4},{6,7},{7,6},{8,9},{9,8},{10,11... | collective-permute-start | bytes 2064392 | tf_op jit(solution)/shard_map/ppermute | solution.py:29
  86.4 6.9 %collective-permute-start.18 = (bf16[2,3,4,16,896]{4,3,2,1,0:T(8,128)(2,1)S(1)}, bf16[2,3,4,16,896]{4,3,2,1,0:T(8,128)(2,1)S(1)}, u32[]{:S(2)}, u32[]{:S(2)}) collective-permute-start(bf16[2,3,4,16,896]{4,3,2,1,0:T(8,128)(2,1)S(1)} %collective-permute-done.15.rest.refs_7_), channel_id=1, source_target_pairs={{0,1},{1,0},{2,3},{3,2},{4,5},{5,4},{6,7},{7,6},{8,9},{9,8},{10,11... | collective-permute-start | bytes 2064392 | tf_op jit(solution)/shard_map/ppermute | solution.py:29
  97.4 15.2 %collective-permute-start.20 = (bf16[2,2,128,1024]{3,2,1,0:T(8,128)(2,1)S(1)}, bf16[2,2,128,1024]{3,2,1,0:T(8,128)(2,1)S(1)}, u32[]{:S(2)}, u32[]{:S(2)}) collective-permute-start(bf16[2,2,128,1024]{3,2,1,0:T(8,128)(2,1)S(1)} %get-tuple-element.38), channel_id=1, source_target_pairs={{0,32},{1,97},{32,0},{33,65},{64,96},{65,33},{96,64},{97,1},{2,34}... | collective-permute-start | bytes 3145736 | tf_op jit(solution)/shard_map/ppermute | solution.py:20
  99.1 7.3 %collective-permute-start.21 = (bf16[3,4,16,896]{3,2,1,0:T(8,128)(2,1)S(1)}, bf16[3,4,16,896]{3,2,1,0:T(8,128)(2,1)S(1)}, u32[]{:S(2)}, u32[]{:S(2)}) collective-permute-start(bf16[3,4,16,896]{3,2,1,0:T(8,128)(2,1)S(1)} %collective-permute-done.16), channel_id=1, source_target_pairs={{0,2},{1,7},{2,0},{3,5},{4,6},{5,3},{6,4},{7,1},{8,10},{9,15},{10,... | collective-permute-start | bytes 1032200 | tf_op jit(solution)/shard_map/ppermute | solution.py:20
  106.5 10.2 %collective-permute-start.23 = (bf16[2,3,4,16,896]{4,3,2,1,0:T(8,128)(2,1)S(1)}, bf16[2,3,4,16,896]{4,3,2,1,0:T(8,128)(2,1)S(1)}, u32[]{:S(2)}, u32[]{:S(2)}) collective-permute-start(bf16[2,3,4,16,896]{4,3,2,1,0:T(8,128)(2,1)S(1)} %pad_maximum_fusion.4.refs_3_), channel_id=1, source_target_pairs={{0,6},{1,3},{2,4},{3,1},{4,2},{5,7},{6,0},{7,5},{8,14},{9,11},{10,... | collective-permute-start | bytes 2064392 | tf_op jit(solution)/shard_map/ppermute | solution.py:20
  113.1 8.6 %collective-permute-start.22 = (bf16[2,128,1024]{2,1,0:T(8,128)(2,1)S(1)}, bf16[2,128,1024]{2,1,0:T(8,128)(2,1)S(1)}, u32[]{:S(2)}, u32[]{:S(2)}) collective-permute-start(bf16[2,128,1024]{2,1,0:T(8,128)(2,1)S(1)} %fusion.3), channel_id=1, source_target_pairs={{0,96},{1,33},{32,64},{33,1},{64,32},{65,97},{96,0},{97,65},{2,98}... | collective-permute-start | bytes 1572872 | tf_op jit(solution)/shard_map/ppermute | solution.py:20
  113.5 16.5 %collective-permute-start.27 = (bf16[2,3,4,16,896]{4,3,2,1,0:T(8,128)(2,1)S(1)}, bf16[2,3,4,16,896]{4,3,2,1,0:T(8,128)(2,1)S(1)}, u32[]{:S(2)}, u32[]{:S(2)}) collective-permute-start(bf16[2,3,4,16,896]{4,3,2,1,0:T(8,128)(2,1)S(1)} %pad_maximum_fusion.4.refs_3_), channel_id=1, source_target_pairs={{0,1},{1,0},{2,3},{3,2},{4,5},{5,4},{6,7},{7,6},{8,9},{9,8},{10,11... | collective-permute-start | bytes 2064392 | tf_op jit(solution)/shard_map/ppermute | solution.py:29
  116.7 13.3 %collective-permute-start.28 = (bf16[2,3,4,16,896]{4,3,2,1,0:T(8,128)(2,1)S(1)}, bf16[2,3,4,16,896]{4,3,2,1,0:T(8,128)(2,1)S(1)}, u32[]{:S(2)}, u32[]{:S(2)}) collective-permute-start(bf16[2,3,4,16,896]{4,3,2,1,0:T(8,128)(2,1)S(1)} %collective-permute-done.23.refs_4_), channel_id=1, source_target_pairs={{0,1},{1,0},{2,3},{3,2},{4,5},{5,4},{6,7},{7,6},{8,9},{9,8},{10,11... | collective-permute-start | bytes 2064392 | tf_op jit(solution)/shard_map/ppermute | solution.py:29
  123.0 13.3 %collective-permute-start.26 = (bf16[32,2048]{1,0:T(8,128)(2,1)S(1)}, bf16[32,2048]{1,0:T(8,128)(2,1)S(1)}, u32[]{:S(2)}, u32[]{:S(2)}) collective-permute-start(bf16[32,2048]{1,0:T(8,128)(2,1)S(1)} %get-tuple-element.61), channel_id=1, source_target_pairs={{0,16},{1,17},{8,24},{9,25},{16,0},{17,1},{24,8},{25,9},{2,18},{3,... | collective-permute-start | bytes 393224 | tf_op jit(solution)/shard_map/ppermute | solution.py:25
  125.5 15.4 %collective-permute-start.25 = (bf16[32,2048]{1,0:T(8,128)(2,1)S(1)}, bf16[32,2048]{1,0:T(8,128)(2,1)S(1)}, u32[]{:S(2)}, u32[]{:S(2)}) collective-permute-start(bf16[32,2048]{1,0:T(8,128)(2,1)S(1)} %get-tuple-element.62), channel_id=1, source_target_pairs={{0,24},{1,9},{8,16},{9,1},{16,8},{17,25},{24,0},{25,17},{2,26},{3,... | collective-permute-start | bytes 393224 | tf_op jit(solution)/shard_map/ppermute | solution.py:20
  130.0 11.0 %collective-permute-start.24 = (bf16[32,2048]{1,0:T(8,128)(2,1)S(1)}, bf16[32,2048]{1,0:T(8,128)(2,1)S(1)}, u32[]{:S(2)}, u32[]{:S(2)}) collective-permute-start(bf16[32,2048]{1,0:T(8,128)(2,1)S(1)} %get-tuple-element.60), channel_id=1, source_target_pairs={{0,8},{1,25},{8,0},{9,17},{16,24},{17,9},{24,16},{25,1},{2,10},{3,... | collective-permute-start | bytes 393224 | tf_op jit(solution)/shard_map/ppermute | solution.py:20
  (9 other events, 87.0 us)
